TPU v7x, 128 devices: a whole 4x4x4 slice. The times are simulated.
128 devices in a mesh: row: 8 (over x, core), col: 16 (over z, y).
Axes of the slice: x: 4, y: 4, z: 4, core: 2. Of those that a mesh axis runs over, the one named last changes fastest.
Arguments:
- matrix: bfloat16 [16384, 16384], P('row', 'col'), may hold values from -6 to 6
- inverses: bfloat16 [2, 512, 512], replicated, may hold values from -0.01171875 to 0.01171875
- adjoint: bfloat16 [64, 16384], P(None, 'col'), may hold values from -0.046875 to 0.046875
- focal_nodes: int32 [64], replicated, may hold values from 0 to 16383
- adjacency: int32 [4, 16384], P(None, ('row', 'col')), may hold values from 0 to 127
- conductance: float32 [4, 16384], P(None, ('row', 'col')), may hold values from 0.25 to 1
Outputs:
- trailing: bfloat16 [16384, 16384], P('row', 'col')
- currents: float32 [64, 16384], P(None, ('row', 'col'))
Inputs may be any that keep to these rules, and one draw needn't show every extreme that they name: `focal_nodes`: each entry is a node index. `adjacency`: each entry is an index within the neighbouring tile.
All inputs are finite; a program needn't handle non-finite values.
Results may differ from a plain program's by a relative error of at most 0.0065.
Values may be sent and summed in bfloat16 or wider, within the bound.
No kernel may reach another device: no remote copies, remote signals or barrier semaphores. Data moves between devices by JAX's collectives and lax.ppermute only.
A program may use at most 64 MiB of HBM per device.

v0:
```python
import jax
import jax.numpy as jnp
from jax import lax
from jax.sharding import PartitionSpec as P


def spread(value, axis, source):
    kept = jnp.where(lax.axis_index(axis) == source, value, 0).astype(value.dtype)
    return lax.psum(kept, axis)


def padded(cells, sides, width):
    for axis, dim in sides:
        count = lax.axis_size(axis)
        ends = count - 1
        head = lax.slice_in_dim(cells, 0, width, axis=dim)
        tail = lax.slice_in_dim(cells, cells.shape[dim] - width, cells.shape[dim], axis=dim)
        cells = jnp.concatenate(
            [
                lax.ppermute(tail, axis, [(i, (i + 1) % count) for i in range(ends)]),
                cells,
                lax.ppermute(head, axis, [((i + 1) % count, i) for i in range(ends)]),
            ],
            axis=dim,
        )
    return cells


def multiply(left, right):
    return jnp.dot(left, right, preferred_element_type=jnp.float32)


def subtract(base, left, right):
    return (base.astype(jnp.float32) - multiply(left, right)).astype(jnp.bfloat16)


def shards(matrix, inverses, adjoint, focal_nodes, adjacency, conductance):
    panel_width = inverses.shape[1]
    trailing = matrix
    for which in range(2):
        offset = which * panel_width
        columns = spread(trailing[:, offset : offset + panel_width], "col", 0)
        upper_rows = spread(trailing[offset : offset + panel_width, :], "row", 0)
        lower_part = multiply(columns, inverses[which]).astype(jnp.bfloat16)
        trailing = subtract(trailing, lower_part, upper_rows)
    sources = adjoint.shape[0]
    width_here = trailing.shape[1]
    col_offset = lax.axis_index("col") * width_here
    positions = col_offset + lax.broadcasted_iota(jnp.int32, (sources, width_here), 1)
    onehot = (positions == focal_nodes[:, None]).astype(jnp.bfloat16)
    stacked = jnp.concatenate([adjoint, onehot], axis=0)
    product = lax.dot_general(
        stacked, trailing, (((1,), (1,)), ((), ())), preferred_element_type=jnp.float32
    )
    partial_sum = product[:sources] + product[sources:]
    injected = lax.psum_scatter(partial_sum, "col", scatter_dimension=1, tiled=True)
    tile_nodes = injected.shape[1]
    halo_grid = padded(injected.reshape(sources, 1, 1, tile_nodes), (("row", 1), ("col", 2)), 1)
    neighbours = jnp.stack(
        [halo_grid[:, 0, 1], halo_grid[:, 2, 1], halo_grid[:, 1, 0], halo_grid[:, 1, 2]]
    )
    node_ids = lax.broadcasted_iota(jnp.int32, (1, 1, tile_nodes), 2)
    selector = (adjacency[:, :, None] == node_ids).astype(jnp.float32)
    gathered = jnp.einsum("ksj,kij->ksi", neighbours, selector, precision=lax.Precision.HIGHEST)
    currents = injected - jnp.sum(conductance[:, None, :] * gathered, axis=0)
    return (trailing, currents)


def solution(mesh):
    placed = (
        P("row", "col"),
        P(),
        P(None, "col"),
        P(),
        P(None, ("row", "col")),
        P(None, ("row", "col")),
    )
    return jax.shard_map(
        shards,
        mesh=mesh,
        in_specs=placed,
        out_specs=(P("row", "col"), P(None, ("row", "col"))),
        check_vma=False,
    )
```

profile of v0, /device:TPU:34, one launch (start us, length us, event | category | flops | bytes accessed | tf_op | source)
XLA Modules:
  0.0 449.8 jit_solution(9729315517777832766)
XLA Ops:
  7.2 0.0 all-reduce.7.cloned.1.call-start
  7.2 2.3 slice_select_fusion.3
  9.5 0.0 all-reduce.7.cloned.1.call-update
  9.5 0.0 all-reduce.5.cloned.1.call-start
  9.6 3.1 slice_select_fusion.1
  12.7 0.0 all-reduce.5.cloned.1.call-update
  12.7 0.0 all-reduce.11.cloned.1.call-start
  12.8 59.7 %all-reduce.7.cloned.1.call-done = bf16[512,1024]{1,0:T(8,128)(2,1)} async-done(((bf16[512,1024]{1,0:T(8,128)(2,1)}), bf16[512,1024]{1,0:T(8,128)(2,1)}) %all-reduce.7.cloned.1.call-update) | async-done | bytes 1048592 | tf_op jit(solution)/shard_map/psum | solution.py:9
  72.5 95.6 %all-reduce.5.cloned.1.call-done = bf16[2048,512]{1,0:T(8,128)(2,1)} async-done(((bf16[2048,512]{1,0:T(8,128)(2,1)}), bf16[2048,512]{1,0:T(8,128)(2,1)}) %all-reduce.5.cloned.1.call-update) | async-done | bytes 2097168 | tf_op jit(solution)/shard_map/psum | solution.py:9
  168.1 8.6 %subtract_convert_fusion.1 = bf16[2048,1024]{1,0:T(8,128)(2,1)} fusion(bf16[2048,1024]{1,0:T(8,128)(2,1)} %param.6, bf16[512,1024]{1,0:T(8,128)(2,1)} %all-reduce.7.cloned.1.call-done, bf16[2048,512]{1,0:T(8,128)(2,1)} %all-reduce.5.cloned.1.call-done, bf16[2,512,512]{2,1,0:T(8,128)(2,1)S(1)} %copy-done.2), kind=kOutput, calls=%fused_computation.1 | convolution fusion | flops 3228565504 | bytes 12058624 | tf_op jit(solution)/shard_map/dot_general | solution.py:30
  176.7 2.3 slice_select_fusion.2
  179.0 0.0 all-reduce.11.cloned.1.call-update
  179.0 0.0 all-reduce.9.cloned.1.call-start
  179.0 3.0 slice_select_fusion
  182.1 0.0 reduce-scatter.2.cloned.1.call-start
  182.2 0.1 compare_convert_fusion
  182.3 56.5 %all-reduce.11.cloned.1.call-done = bf16[512,1024]{1,0:T(8,128)(2,1)} async-done(((bf16[512,1024]{1,0:T(8,128)(2,1)}), bf16[512,1024]{1,0:T(8,128)(2,1)}) %all-reduce.11.cloned.1.call-update) | async-done | bytes 1048592 | tf_op jit(solution)/shard_map/psum | solution.py:9
  238.8 95.2 %all-reduce.9.cloned.1.call-done = bf16[2048,512]{1,0:T(8,128)(2,1)} async-done(((bf16[2048,512]{1,0:T(8,128)(2,1)}), bf16[2048,512]{1,0:T(8,128)(2,1)}) %all-reduce.9.cloned.1.call-update) | async-done | bytes 2097168 | tf_op jit(solution)/shard_map/psum | solution.py:9
  334.0 8.6 %subtract_convert_fusion = bf16[2048,1024]{1,0:T(8,128)(2,1)} fusion(bf16[2048,1024]{1,0:T(8,128)(2,1)} %subtract_convert_fusion.1, bf16[512,1024]{1,0:T(8,128)(2,1)} %all-reduce.11.cloned.1.call-done, bf16[2048,512]{1,0:T(8,128)(2,1)} %all-reduce.9.cloned.1.call-done, bf16[2,512,512]{2,1,0:T(8,128)(2,1)S(1)} %copy-done.2), kind=kOutput, calls=%fused_computation | convolution fusion | flops 3228565504 | bytes 12058624 | tf_op jit(solution)/shard_map/dot_general | solution.py:30
  342.6 3.7 fusion.9
  346.4 0.8 slice_add_fusion
  347.3 71.9 %reduce-scatter.2.cloned.1.call-done = f32[64,128]{1,0:T(8,128)} async-done(((f32[64,2048]{1,0:T(8,128)}), f32[64,128]{1,0:T(8,128)}) %reduce-scatter.2.cloned.1.call-update) | async-done | bytes 32784 | tf_op jit(solution)/shard_map/reduce_scatter | solution.py:56
  419.2 1.9 collective-permute-start
  421.1 3.6 collective-permute-start.1
  424.7 1.9 collective-permute-done.1
  426.6 0.8 pad_maximum_fusion
  427.4 4.6 %collective-permute-start.3 = (f32[64,3,1,128]{3,0,2,1:T(8,128)S(1)}, f32[64,3,1,128]{3,0,2,1:T(8,128)S(1)}, u32[]{:S(2)}, u32[]{:S(2)}) collective-permute-start(f32[64,3,1,128]{3,0,2,1:T(8,128)S(1)} %pad_maximum_fusion), channel_id=1, source_target_pairs={{1,0},{2,1},{3,2},{4,3},{5,4},{6,5},{7,6},{8,7},{9,8},{10,9},{11,1... | collective-permute-start | bytes 294920 | tf_op jit(solution)/shard_map/ppermute | solution.py:22
  432.0 1.9 collective-permute-start.2
  433.9 0.8 collective-permute-done.3
  434.7 6.7 %collective-permute-done.2 = f32[64,3,1,128]{3,0,2,1:T(8,128)S(1)} collective-permute-done((f32[64,3,1,128]{3,0,2,1:T(8,128)S(1)}, f32[64,3,1,128]{3,0,2,1:T(8,128)S(1)}, u32[]{:S(2)}, u32[]{:S(2)}) %collective-permute-start.2) | collective-permute-done | bytes 98336 | tf_op jit(solution)/shard_map/ppermute | solution.py:20
  441.4 0.4 fusion
  441.9 1.4 sub.11
  (16 shorter events, 0.1 us)
Async XLA Ops:
  7.2 65.3 %all-reduce.7.cloned.1.call-start = ((), (), s32[]{:S(2)}) async-start(), calls=%async_computation.2 | async-start | bytes 2097152 | tf_op jit(solution)/shard_map/psum | solution.py:9
  9.5 158.6 %copy-start.2 = (bf16[2,512,512]{2,1,0:T(8,128)(2,1)S(1)}, bf16[2,512,512]{2,1,0:T(8,128)(2,1)}, u32[]{:S(2)}) copy-start(bf16[2,512,512]{2,1,0:T(8,128)(2,1)} %param.7) | copy-start | bytes 3145732
  9.5 158.5 %all-reduce.5.cloned.1.call-start = ((), (), s32[]{:S(2)}) async-start(), calls=%async_computation.1 | async-start | bytes 4194304 | tf_op jit(solution)/shard_map/psum | solution.py:9
  12.7 226.1 %all-reduce.11.cloned.1.call-start = ((), (), s32[]{:S(2)}) async-start(), calls=%async_computation.4 | async-start | bytes 2097152 | tf_op jit(solution)/shard_map/psum | solution.py:9
  179.0 3.2 copy-start.1
  179.0 155.0 %all-reduce.9.cloned.1.call-start = ((), (), s32[]{:S(2)}) async-start(), calls=%async_computation.3 | async-start | bytes 4194304 | tf_op jit(solution)/shard_map/psum | solution.py:9
  182.1 237.0 %reduce-scatter.2.cloned.1.call-start = ((), (), s32[]{:S(2)}) async-start(), calls=%async_computation.5 | async-start | bytes 557056 | tf_op jit(solution)/shard_map/reduce_scatter | solution.py:56
  182.3 160.3 %copy-start = (bf16[64,1024]{1,0:T(8,128)(2,1)S(1)}, bf16[64,1024]{1,0:T(8,128)(2,1)}, u32[]{:S(2)}) copy-start(bf16[64,1024]{1,0:T(8,128)(2,1)} %param.8) | copy-start | bytes 393220
  342.6 98.8 %copy-start.3 = (s32[4,128]{1,0:T(4,128)S(1)}, s32[4,128]{1,0:T(4,128)}, u32[]{:S(2)}) copy-start(s32[4,128]{1,0:T(4,128)} %param.10) | copy-start | bytes 6148
  342.6 98.8 %copy-start.4 = (f32[4,128]{1,0:T(4,128)S(1)}, f32[4,128]{1,0:T(4,128)}, u32[]{:S(2)}) copy-start(f32[4,128]{1,0:T(4,128)} %param.11) | copy-start | bytes 6148
  419.2 5.6 %collective-permute-start = (f32[64,1,1,128]{3,0,2,1:T(8,128)}, f32[64,1,1,128]{3,0,2,1:T(8,128)S(1)}, u32[]{:S(2)}, u32[]{:S(2)}) collective-permute-start(f32[64,1,1,128]{3,0,2,1:T(8,128)} %bitcast.20), channel_id=1, source_target_pairs={{0,16},{16,32},{32,48},{48,64},{64,80},{80,96},{96,112},{1,17},{17... | collective-permute-start | bytes 98312 | tf_op jit(solution)/shard_map/ppermute | solution.py:20
  421.1 5.5 %collective-permute-start.1 = (f32[64,1,1,128]{3,0,2,1:T(8,128)}, f32[64,1,1,128]{3,0,2,1:T(8,128)S(1)}, u32[]{:S(2)}, u32[]{:S(2)}) collective-permute-start(f32[64,1,1,128]{3,0,2,1:T(8,128)} %bitcast.21), channel_id=1, source_target_pairs={{16,0},{32,16},{48,32},{64,48},{80,64},{96,80},{112,96},{17,1},{33... | collective-permute-start | bytes 98312 | tf_op jit(solution)/shard_map/ppermute | solution.py:22
  427.4 7.3 %collective-permute-start.3 = (f32[64,3,1,128]{3,0,2,1:T(8,128)S(1)}, f32[64,3,1,128]{3,0,2,1:T(8,128)S(1)}, u32[]{:S(2)}, u32[]{:S(2)}) collective-permute-start(f32[64,3,1,128]{3,0,2,1:T(8,128)S(1)} %pad_maximum_fusion), channel_id=1, source_target_pairs={{1,0},{2,1},{3,2},{4,3},{5,4},{6,5},{7,6},{8,7},{9,8},{10,9},{11,1... | collective-permute-start | bytes 294920 | tf_op jit(solution)/shard_map/ppermute | solution.py:22
  432.0 9.4 %collective-permute-start.2 = (f32[64,3,1,128]{3,0,2,1:T(8,128)S(1)}, f32[64,3,1,128]{3,0,2,1:T(8,128)S(1)}, u32[]{:S(2)}, u32[]{:S(2)}) collective-permute-start(f32[64,3,1,128]{3,0,2,1:T(8,128)S(1)} %pad_maximum_fusion), channel_id=1, source_target_pairs={{0,1},{1,2},{2,3},{3,4},{4,5},{5,6},{6,7},{7,8},{8,9},{9,10},{10,1... | collective-permute-start | bytes 294920 | tf_op jit(solution)/shard_map/ppermute | solution.py:20
Sparse Core Ops, SparseCore 0:
  10.3 62.0 all-reduce.6
  76.4 91.6 all-reduce.4
  179.1 59.6 all-reduce.10
  242.4 91.6 all-reduce.8
  347.4 71.7 reduce-scatter.1
where the time goes:
time: 451 us; the launch traced here: 450 us
  waiting for transfers between devices  388 us (86%)
  matrix products  21.4 us (5%)
  between operations  13.9 us (3%)
  other arithmetic  13.8 us (3%)
  starting transfers between devices  12.2 us (3%)
    psum x4, waiting for transfers between devices, spread(): return lax.psum(kept, axis)  307 us
    reduce_scatter x1, waiting for transfers between devices, shards(): lax.psum_scatter(partial_sum, 'col', scatter_dimension=1, tiled=True)  71.9 us
    dot_general x2, matrix products, multiply(): return jnp.dot(left, right, preferred_element_type=jnp.float32)  17.2 us
    select_n x4, other arithmetic, spread(): jnp.where(lax.axis_index(axis) == source, value, 0).astype(value.dtype)  10.8 us
  transfers between devices with their start and end apart: 9, of which 8 were waited for; matrix products, arithmetic and copies ran while one was open for 1% of the time, Pallas kernels for 0%

commit v1 on v0

v1 whole, which is shorter than its diff:
```python
import functools

import jax
import jax.numpy as jnp
from jax import lax
from jax.experimental import pallas as pl
from jax.experimental.pallas import tpu as pltpu
from jax.sharding import PartitionSpec as P

BF16 = jnp.bfloat16
F32 = jnp.float32


def multiply(left, right):
    return jnp.dot(left, right, preferred_element_type=F32)


def spread_rows(value, row):
    away = [lax.ppermute(value, "row", [(0, at)]) for at in (2, 6, 4)]
    even = jnp.where(row == 0, value, away[0] + away[1] + away[2])
    other = lax.ppermute(even, "row", [(at, at + 1) for at in range(0, 8, 2)])
    return jnp.where(row % 2 == 0, even, other)


def scatter_cols(pieces, col):
    count = pieces.shape[0]
    got = jnp.where(col == 0, pieces[0], jnp.zeros_like(pieces[0]))
    for at in range(1, count):
        got = got + lax.ppermute(pieces[at], "col", [(0, at)])
    return got


def update_kernel(base_ref, low_ref, up0_ref, up1_ref, stacked_ref, out_ref, part_ref):
    half = up0_ref.shape[0]
    sources = part_ref.shape[0]
    low = low_ref[0]
    lifted = multiply(low[:, :half], up0_ref[...]) + multiply(low[:, half:], up1_ref[...])
    done = (base_ref[...].astype(F32) - lifted).astype(BF16)
    out_ref[...] = done
    product = lax.dot_general(
        stacked_ref[...], done, (((1,), (1,)), ((), ())), preferred_element_type=F32
    )
    part_ref[...] = product[:sources] + product[sources:]


def update(base, low, up0, up1, stacked):
    tiles = low.shape[0]
    rows, width = base.shape
    step = rows // tiles
    depth = low.shape[2]
    sources = stacked.shape[0] // 2
    whole = lambda i: (0, 0)
    return pl.pallas_call(
        update_kernel,
        grid=(tiles,),
        in_specs=[
            pl.BlockSpec((step, width), lambda i: (i, 0)),
            pl.BlockSpec((1, step, depth), lambda i: (i, 0, 0)),
            pl.BlockSpec(up0.shape, whole),
            pl.BlockSpec(up1.shape, whole),
            pl.BlockSpec(stacked.shape, whole),
        ],
        out_specs=[
            pl.BlockSpec((step, width), lambda i: (i, 0)),
            pl.BlockSpec((sources, step), lambda i: (0, i)),
        ],
        out_shape=[
            jax.ShapeDtypeStruct((rows, width), BF16),
            jax.ShapeDtypeStruct((sources, rows), F32),
        ],
        compiler_params=pltpu.CompilerParams(vmem_limit_bytes=32 << 20),
    )(base, low, up0, up1, stacked)


def shards(matrix, inverses, adjoint, focal_nodes, adjacency, conductance):
    row, col = lax.axis_index("row"), lax.axis_index("col")
    cols = lax.axis_size("col")
    panel = inverses.shape[1]
    both = 2 * panel
    sources = adjoint.shape[0]
    rows_here, width_here = matrix.shape

    panels = matrix[:, :both]
    upper = matrix[:both]
    corner01 = spread_rows(upper[:panel, panel:both], row)
    corner10 = spread_rows(upper[panel:, :panel], row)
    up0 = spread_rows(upper[:panel], row)
    up1 = spread_rows(upper[panel:], row)

    low0 = multiply(panels[:, :panel], inverses[0]).astype(BF16)
    piece0 = scatter_cols(low0.reshape(cols, -1, panel), col)

    second = (panels[:, panel:].astype(F32) - multiply(low0, corner01)).astype(BF16)
    low1 = multiply(second, inverses[1]).astype(BF16)
    cross = multiply(corner10, inverses[0]).astype(BF16)
    joined = jnp.concatenate([low1.reshape(cols, -1, panel), cross.reshape(cols, -1, panel)], axis=1)
    piece1 = scatter_cols(joined, col)

    tile = rows_here // cols
    share = panel // cols // 2
    cross_piece = jnp.concatenate([piece1[tile : tile + share], piece1[tile + share :]], axis=1)
    piece = jnp.concatenate(
        [jnp.concatenate([piece0, piece1[:tile]], axis=1), cross_piece], axis=0
    )
    low = lax.all_gather(piece, "col")
    crossed = low[:, tile:]
    cross_all = jnp.stack([crossed[:, :, :panel], crossed[:, :, panel:]], axis=1).reshape(panel, panel)
    up1 = (up1.astype(F32) - multiply(cross_all, up0)).astype(BF16)

    positions = col * width_here + lax.broadcasted_iota(jnp.int32, (sources, width_here), 1)
    onehot = (positions == focal_nodes[:, None]).astype(BF16)
    stacked = jnp.concatenate([adjoint, onehot], axis=0)
    trailing, partial_sum = update(matrix, low, up0, up1, stacked)

    swapped = lax.all_to_all(
        partial_sum.reshape(sources, cols, tile), "col", split_axis=1, concat_axis=0, tiled=True
    )
    injected = jnp.sum(swapped.reshape(cols, sources, tile), axis=0)

    count_row = lax.axis_size("row")
    neighbours = jnp.stack(
        [
            lax.ppermute(injected, "row", [(i, i + 1) for i in range(count_row - 1)]),
            lax.ppermute(injected, "row", [(i + 1, i) for i in range(count_row - 1)]),
            lax.ppermute(injected, "col", [(i, i + 1) for i in range(cols - 1)]),
            lax.ppermute(injected, "col", [(i + 1, i) for i in range(cols - 1)]),
        ]
    )
    node_ids = lax.broadcasted_iota(jnp.int32, (1, 1, tile), 2)
    selector = (adjacency[:, :, None] == node_ids).astype(F32)
    gathered = jnp.einsum("ksj,kij->ksi", neighbours, selector, precision=lax.Precision.HIGHEST)
    currents = injected - jnp.sum(conductance[:, None, :] * gathered, axis=0)
    return (trailing, currents)


def solution(mesh):
    placed = (
        P("row", "col"),
        P(),
        P(None, "col"),
        P(),
        P(None, ("row", "col")),
        P(None, ("row", "col")),
    )
    return jax.shard_map(
        shards,
        mesh=mesh,
        in_specs=placed,
        out_specs=(P("row", "col"), P(None, ("row", "col"))),
        check_vma=False,
    )
```

time: 451 us -> 254 us (0.56)
  the two profiles are of different devices: /device:TPU:34 before, /device:TPU:28 now
where the time goes in v1:
time: 254 us; the launch traced here: 253 us
  waiting for transfers between devices  100 us (39%)
  starting transfers between devices  58.1 us (23%)
  blocking collectives  23.8 us (9%)
  other arithmetic  17.2 us (7%)
  between operations  14.9 us (6%)
  local copies, waits for them, and re-layouts  14.5 us (6%)
  matrix products  12.5 us (5%)
  Pallas kernels  11.6 us (5%)
    ppermute x12, waiting for transfers between devices, spread_rows(): away = [lax.ppermute(value, 'row', [(0, at)]) for at in (2, 6, 4)]  66.4 us
    ppermute x30, starting transfers between devices, scatter_cols(): got = got + lax.ppermute(pieces[at], 'col', [(0, at)])  26.9 us
    all_to_all x1, blocking collectives, shards(): lax.all_to_all(partial_sum.reshape(sources, cols, tile), 'col', split_axi...  23.8 us
    all_gather x1, waiting for transfers between devices, shards(): low = lax.all_gather(piece, 'col')  14.8 us
    ppermute x30, waiting for transfers between devices, scatter_cols(): got = got + lax.ppermute(pieces[at], 'col', [(0, at)])  13.4 us
    dot_general x4, matrix products, multiply(): return jnp.dot(left, right, preferred_element_type=F32)  12 us
    ppermute x12, starting transfers between devices, spread_rows(): away = [lax.ppermute(value, 'row', [(0, at)]) for at in (2, 6, 4)]  11.9 us
    pallas_call x1, Pallas kernels, update(): pl.pallas_call(update_kernel, grid=(tiles,), in_specs=[pl.BlockSpec((step...  11.6 us
  transfers between devices with their start and end apart: 51, of which 8 were waited for; matrix products, arithmetic and copies ran while one was open for 12% of the time, Pallas kernels for 0%

profile of v1, /device:TPU:28, one launch (start us, length us, event | category | flops | bytes accessed | tf_op | source)
XLA Modules:
  0.0 252.6 jit_solution(4792954523713685514)
XLA Ops:
  11.0 13.9 %collective-permute-done.17 = bf16[512,512]{1,0:T(8,128)(2,1)S(1)} collective-permute-done((bf16[512,512]{1,0:T(8,128)(2,1)S(1)}, bf16[512,512]{1,0:T(8,128)(2,1)S(1)}, u32[]{:S(2)}, u32[]{:S(2)}) %collective-permute-start.17) | collective-permute-done | bytes 524320 | tf_op jit(solution)/shard_map/ppermute | solution.py:19
  25.0 2.1 add_select_fusion.3
  27.8 1.5 collective-permute-start.20
  30.5 3.0 %convolution_convert_fusion.1 = bf16[2048,512]{0,1:T(8,128)(2,1)S(1)} fusion(bf16[2048,1024]{1,0:T(8,128)(2,1)} %base_ref.1, bf16[2,512,512]{2,1,0:T(8,128)(2,1)} %param.7), kind=kOutput, calls=%fused_computation.32 | convolution fusion | flops 1074790400 | bytes 4718592 | tf_op jit(solution)/shard_map/dot_general | solution.py:15
  33.5 2.1 collective-permute-start.18
  39.0 3.1 %collective-permute-done.21 = bf16[512,512]{1,0:T(8,128)(2,1)} collective-permute-done((bf16[512,512]{1,0:T(8,128)(2,1)}, bf16[512,512]{1,0:T(8,128)(2,1)}, u32[]{:S(2)}, u32[]{:S(2)}) %collective-permute-start.21) | collective-permute-done | bytes 524320 | tf_op jit(solution)/shard_map/ppermute | solution.py:19
  43.4 2.3 add_select_fusion.2
  46.4 2.1 collective-permute-start.22
  48.5 5.4 %convolution_convert_fusion = bf16[2048,512]{1,0:T(8,128)(2,1)} fusion(bf16[2048,512]{0,1:T(8,128)(2,1)S(1)} %convolution_convert_fusion.1, bf16[2048,1024]{1,0:T(8,128)(2,1)} %base_ref.1, bf16[2,512,512]{2,1,0:T(8,128)(2,1)} %param.7, bf16[512,512]{1,0:T(8,128)(2,1)S(1)} %get-tuple-element.25, bf16[512,512]{1,0:T(8,128)(2,1)} %collective-permute-done.18, ...), kind=kOutput, calls=%fused_computation.31 | convolution fusion | flops 2151940096 | bytes 7864321 | tf_op jit(solution)/shard_map/dot_general | solution.py:15
  53.8 3.0 %copy.21 = bf16[16,128,512]{1,2,0:T(8,128)(2,1)S(1)} copy(bf16[16,128,512]{2,1,0:T(8,128)(2,1)} %bitcast.88) | data formatting | bytes 4194304 | tf_op jit(solution)/shard_map/reshape | solution.py:96
  62.2 1.6 convolution_convert_fusion.2
  63.9 1.7 copy.22
  67.1 5.8 %collective-permute-done.2 = bf16[128,512]{0,1:T(8,128)(2,1)S(1)} collective-permute-done((bf16[128,512]{0,1:T(8,128)(2,1)}, bf16[128,512]{0,1:T(8,128)(2,1)S(1)}, u32[]{:S(2)}, u32[]{:S(2)}) %collective-permute-start.2) | collective-permute-done | bytes 131104 | tf_op jit(solution)/shard_map/ppermute | solution.py:29
  75.0 2.7 %fusion.54 = (bf16[160,512]{0,1:T(8,128)(2,1)S(1)}, bf16[160,512]{0,1:T(8,128)(2,1)S(1)}, bf16[160,512]{0,1:T(8,128)(2,1)S(1)}, bf16[160,512]{0,1:T(8,128)(2,1)S...) fusion(bf16[16,32,512]{1,2,0:T(8,128)(2,1)} %copy.22, ...), kind=kLoop, calls=%fused_computation.103 | loop fusion | flops 2949120 | bytes 4096000 | tf_op jit(solution)/shard_map/squeeze | solution.py:29
  87.2 7.5 %collective-permute-done.25 = bf16[160,512]{0,1:T(8,128)(2,1)S(1)} collective-permute-done((bf16[160,512]{0,1:T(8,128)(2,1)S(1)}, bf16[160,512]{0,1:T(8,128)(2,1)S(1)}, u32[]{:S(2)}, u32[]{:S(2)}) %collective-permute-start.25) | collective-permute-done | bytes 163872 | tf_op jit(solution)/shard_map/ppermute | solution.py:29
  102.3 1.7 add_add_fusion.1
  104.0 1.9 add_add_fusion
  111.2 27.5 %collective-permute-done.44 = bf16[512,1024]{1,0:T(8,128)(2,1)S(1)} collective-permute-done((bf16[512,1024]{1,0:T(8,128)(2,1)S(1)}, bf16[512,1024]{1,0:T(8,128)(2,1)S(1)}, u32[]{:S(2)}, u32[]{:S(2)}) %collective-permute-start.44) | collective-permute-done | bytes 1048608 | tf_op jit(solution)/shard_map/ppermute | solution.py:19
  138.8 2.8 %add_select_fusion = (bf16[512,1024]{1,0:T(8,128)(2,1)}, bf16[512,1024]{1,0:T(8,128)(2,1)S(1)}) fusion(bf16[512,1024]{1,0:T(8,128)(2,1)S(1)} %collective-permute-done.44, bf16[512,1024]{1,0:T(8,128)(2,1)S(1)} %collective-permute-done.42, bf16[512,1024]{1,0:T(8,128)(2,1)S(1)} %collective-permute-done.43, pred[]{:T(512)S(6)} %eq.44, bf16[2048,1024]{1,0:T(8,128)(2,1)} %base_ref.1), kind=kLoop, calls=%fused_computation.38 | loop fusion | flops 1572864 | bytes 7340033 | tf_op jit(solution)/shard_map/jit(_where)/select_n | solution.py:20
  144.6 21.9 %collective-permute-done.40 = bf16[512,1024]{1,0:T(8,128)(2,1)S(1)} collective-permute-done((bf16[512,1024]{1,0:T(8,128)(2,1)S(1)}, bf16[512,1024]{1,0:T(8,128)(2,1)S(1)}, u32[]{:S(2)}, u32[]{:S(2)}) %collective-permute-start.40) | collective-permute-done | bytes 1048608 | tf_op jit(solution)/shard_map/ppermute | solution.py:19
  166.5 1.5 add_select_fusion.1
  169.3 2.3 collective-permute-start.45
  171.9 14.8 %all-gather.3.cloned.1.call-done = bf16[2304,1024]{1,0:T(8,128)(2,1)} async-done(((bf16[144,1024]{1,0:T(8,128)(2,1)}), bf16[2304,1024]{1,0:T(8,128)(2,1)}) %all-gather.3.cloned.1.call-update) | async-done | bytes 4718608 | tf_op jit(solution)/shard_map/all_gather | solution.py:105
  188.0 2.0 subtract_convert_fusion.1.up1_ref
  190.0 2.3 copy-done.1
  192.3 11.6 %shard_map.77 = (bf16[2048,1024]{1,0:T(8,128)(2,1)}, f32[64,2048]{1,0:T(8,128)S(1)}) custom-call(bf16[2048,1024]{1,0:T(8,128)(2,1)S(1)} %copy-done, bf16[16,144,1024]{2,1,0:T(8,128)(2,1)S(1)} %bitcast.87, bf16[512,1024]{1,0:T(8,128)(2,1)S(1)} %broadcast_select_fusion.up0_ref, bf16[512,1024]{1,0:T(8,128)(2,1)S(1)} %subtract_convert_fusion.1.up1_ref, ...), custom_call_target="tpu_custom_call" | custom-call | tf_op jit(solution)/shard_map/pallas_call | solution.py:53
  204.0 23.8 %all_to_all.4 = f32[64,16,128]{2,0,1:T(8,128)S(1)} all-to-all(f32[64,16,128]{2,0,1:T(8,128)S(1)} %copy_bitcast_fusion), channel_id=1, replica_groups=mesh['row'=8,'col'=16] {'col'}, dimensions={1} | all-to-all | bytes 1048576 | tf_op jit(solution)/shard_map/all_to_all | solution.py:115
  227.8 1.9 collective-permute-start.46
  229.7 3.6 %collective-permute-start.47 = (f32[64,128]{1,0:T(8,128)S(1)}, f32[64,128]{1,0:T(8,128)S(1)}, u32[]{:S(2)}, u32[]{:S(2)}) collective-permute-start(f32[64,128]{1,0:T(8,128)S(1)} %reduce_sum.18), channel_id=1, source_target_pairs={{16,0},{32,16},{48,32},{64,48},{80,64},{96,80},{112,96},{17,1},{33... | collective-permute-start | bytes 98312 | tf_op jit(solution)/shard_map/ppermute | solution.py:124
  233.4 3.4 %collective-permute-start.48 = (f32[64,128]{1,0:T(8,128)S(1)}, f32[64,128]{1,0:T(8,128)S(1)}, u32[]{:S(2)}, u32[]{:S(2)}) collective-permute-start(f32[64,128]{1,0:T(8,128)S(1)} %reduce_sum.18), channel_id=1, source_target_pairs={{0,1},{1,2},{2,3},{3,4},{4,5},{5,6},{6,7},{7,8},{8,9},{9,10},{10,1... | collective-permute-start | bytes 98312 | tf_op jit(solution)/shard_map/ppermute | solution.py:125
  236.8 2.4 collective-permute-start.49
  239.3 5.4 %collective-permute-done.49 = f32[64,128]{1,0:T(8,128)S(1)} collective-permute-done((f32[64,128]{1,0:T(8,128)S(1)}, f32[64,128]{1,0:T(8,128)S(1)}, u32[]{:S(2)}, u32[]{:S(2)}) %collective-permute-start.49) | collective-permute-done | bytes 32800 | tf_op jit(solution)/shard_map/ppermute | solution.py:126
  (143 shorter events, 49.1 us)
Async XLA Ops:
  7.2 179.5 %all-gather.3.cloned.1.call-start = ((), (), s32[]{:S(2)}) async-start(), calls=%async_computation.1 | async-start | bytes 5013504 | tf_op jit(solution)/shard_map/all_gather | solution.py:105
  9.7 15.3 %collective-permute-start.17 = (bf16[512,512]{1,0:T(8,128)(2,1)S(1)}, bf16[512,512]{1,0:T(8,128)(2,1)S(1)}, u32[]{:S(2)}, u32[]{:S(2)}) collective-permute-start(bf16[512,512]{1,0:T(8,128)(2,1)S(1)} %slice.179), channel_id=1, source_target_pairs={{0,64},{1,65},{2,66},{3,67},{4,68},{5,69},{6,70},{7,71},{8,72},{9,... | collective-permute-start | bytes 1572872 | tf_op jit(solution)/shard_map/ppermute | solution.py:19
  27.1 10.6 %collective-permute-start.19 = (bf16[512,512]{1,0:T(8,128)(2,1)}, bf16[512,512]{1,0:T(8,128)(2,1)S(1)}, u32[]{:S(2)}, u32[]{:S(2)}) collective-permute-start(bf16[512,512]{1,0:T(8,128)(2,1)} %get-tuple-element.26), channel_id=1, source_target_pairs={{0,32},{1,33},{2,34},{3,35},{4,36},{5,37},{6,38},{7,39},{8,40},{9,... | collective-permute-start | bytes 1572872 | tf_op jit(solution)/shard_map/ppermute | solution.py:19
  27.8 10.6 %collective-permute-start.20 = (bf16[512,512]{1,0:T(8,128)(2,1)}, bf16[512,512]{1,0:T(8,128)(2,1)}, u32[]{:S(2)}, u32[]{:S(2)}) collective-permute-start(bf16[512,512]{1,0:T(8,128)(2,1)} %get-tuple-element.26), channel_id=1, source_target_pairs={{0,96},{1,97},{2,98},{3,99},{4,100},{5,101},{6,102},{7,103},{8,104... | collective-permute-start | bytes 1572872 | tf_op jit(solution)/shard_map/ppermute | solution.py:19
  29.2 12.9 %collective-permute-start.21 = (bf16[512,512]{1,0:T(8,128)(2,1)}, bf16[512,512]{1,0:T(8,128)(2,1)}, u32[]{:S(2)}, u32[]{:S(2)}) collective-permute-start(bf16[512,512]{1,0:T(8,128)(2,1)} %get-tuple-element.26), channel_id=1, source_target_pairs={{0,64},{1,65},{2,66},{3,67},{4,68},{5,69},{6,70},{7,71},{8,72},{9,... | collective-permute-start | bytes 1572872 | tf_op jit(solution)/shard_map/ppermute | solution.py:19
  33.5 12.9 %collective-permute-start.18 = (bf16[512,512]{1,0:T(8,128)(2,1)S(1)}, bf16[512,512]{1,0:T(8,128)(2,1)}, u32[]{:S(2)}, u32[]{:S(2)}) collective-permute-start(bf16[512,512]{1,0:T(8,128)(2,1)S(1)} %get-tuple-element.25), channel_id=1, source_target_pairs={{0,16},{32,48},{64,80},{96,112},{1,17},{33,49},{65,81},{97,113},{2... | collective-permute-start | bytes 1572872 | tf_op jit(solution)/shard_map/ppermute | solution.py:21
  37.0 8.7 %collective-permute-start = (bf16[128,512]{0,1:T(8,128)(2,1)}, bf16[128,512]{0,1:T(8,128)(2,1)S(1)}, u32[]{:S(2)}, u32[]{:S(2)}) collective-permute-start(bf16[128,512]{0,1:T(8,128)(2,1)} %get-tuple-element.27), channel_id=1, source_target_pairs={{0,1},{16,17},{32,33},{48,49},{64,65},{80,81},{96,97},{112,113}} | collective-permute-start | bytes 393224 | tf_op jit(solution)/shard_map/ppermute | solution.py:29
  37.7 19.2 %collective-permute-start.1 = (bf16[128,512]{0,1:T(8,128)(2,1)}, bf16[128,512]{0,1:T(8,128)(2,1)S(1)}, u32[]{:S(2)}, u32[]{:S(2)}) collective-permute-start(bf16[128,512]{0,1:T(8,128)(2,1)} %get-tuple-element.41), channel_id=1, source_target_pairs={{0,2},{16,18},{32,34},{48,50},{64,66},{80,82},{96,98},{112,114}} | collective-permute-start | bytes 393224 | tf_op jit(solution)/shard_map/ppermute | solution.py:29
  38.4 19.2 %collective-permute-start.10 = (bf16[128,512]{0,1:T(8,128)(2,1)}, bf16[128,512]{0,1:T(8,128)(2,1)S(1)}, u32[]{:S(2)}, u32[]{:S(2)}) collective-permute-start(bf16[128,512]{0,1:T(8,128)(2,1)} %get-tuple-element.32), channel_id=1, source_target_pairs={{0,11},{16,27},{32,43},{48,59},{64,75},{80,91},{96,107},{112,123}} | collective-permute-start | bytes 393224 | tf_op jit(solution)/shard_map/ppermute | solution.py:29
  42.1 16.2 %collective-permute-start.11 = (bf16[128,512]{0,1:T(8,128)(2,1)}, bf16[128,512]{0,1:T(8,128)(2,1)}, u32[]{:S(2)}, u32[]{:S(2)}) collective-permute-start(bf16[128,512]{0,1:T(8,128)(2,1)} %get-tuple-element.31), channel_id=1, source_target_pairs={{0,12},{16,28},{32,44},{48,60},{64,76},{80,92},{96,108},{112,124}} | collective-permute-start | bytes 393224 | tf_op jit(solution)/shard_map/ppermute | solution.py:29
  45.7 13.9 %collective-permute-start.12 = (bf16[128,512]{0,1:T(8,128)(2,1)}, bf16[128,512]{0,1:T(8,128)(2,1)S(1)}, u32[]{:S(2)}, u32[]{:S(2)}) collective-permute-start(bf16[128,512]{0,1:T(8,128)(2,1)} %get-tuple-element.30), channel_id=1, source_target_pairs={{0,13},{16,29},{32,45},{48,61},{64,77},{80,93},{96,109},{112,125}} | collective-permute-start | bytes 393224 | tf_op jit(solution)/shard_map/ppermute | solution.py:29
  46.4 14.6 %collective-permute-start.22 = (bf16[512,512]{1,0:T(8,128)(2,1)}, bf16[512,512]{1,0:T(8,128)(2,1)}, u32[]{:S(2)}, u32[]{:S(2)}) collective-permute-start(bf16[512,512]{1,0:T(8,128)(2,1)} %add_select_fusion.2), channel_id=1, source_target_pairs={{0,16},{32,48},{64,80},{96,112},{1,17},{33,49},{65,81},{97,113},{2... | collective-permute-start | bytes 1572872 | tf_op jit(solution)/shard_map/ppermute | solution.py:21
  56.9 8.7 %collective-permute-start.13 = (bf16[128,512]{0,1:T(8,128)(2,1)}, bf16[128,512]{0,1:T(8,128)(2,1)S(1)}, u32[]{:S(2)}, u32[]{:S(2)}) collective-permute-start(bf16[128,512]{0,1:T(8,128)(2,1)} %get-tuple-element.29), channel_id=1, source_target_pairs={{0,14},{16,30},{32,46},{48,62},{64,78},{80,94},{96,110},{112,126}} | collective-permute-start | bytes 393224 | tf_op jit(solution)/shard_map/ppermute | solution.py:29
  57.6 8.8 %collective-permute-start.14 = (bf16[128,512]{0,1:T(8,128)(2,1)}, bf16[128,512]{0,1:T(8,128)(2,1)S(1)}, u32[]{:S(2)}, u32[]{:S(2)}) collective-permute-start(bf16[128,512]{0,1:T(8,128)(2,1)} %get-tuple-element.28), channel_id=1, source_target_pairs={{0,15},{16,31},{32,47},{48,63},{64,79},{80,95},{96,111},{112,127}} | collective-permute-start | bytes 393224 | tf_op jit(solution)/shard_map/ppermute | solution.py:29
  58.3 14.7 %collective-permute-start.2 = (bf16[128,512]{0,1:T(8,128)(2,1)}, bf16[128,512]{0,1:T(8,128)(2,1)S(1)}, u32[]{:S(2)}, u32[]{:S(2)}) collective-permute-start(bf16[128,512]{0,1:T(8,128)(2,1)} %get-tuple-element.40), channel_id=1, source_target_pairs={{0,3},{16,19},{32,35},{48,51},{64,67},{80,83},{96,99},{112,115}} | collective-permute-start | bytes 393224 | tf_op jit(solution)/shard_map/ppermute | solution.py:29
  59.6 14.0 %collective-permute-start.3 = (bf16[128,512]{0,1:T(8,128)(2,1)}, bf16[128,512]{0,1:T(8,128)(2,1)}, u32[]{:S(2)}, u32[]{:S(2)}) collective-permute-start(bf16[128,512]{0,1:T(8,128)(2,1)} %get-tuple-element.39), channel_id=1, source_target_pairs={{0,4},{16,20},{32,36},{48,52},{64,68},{80,84},{96,100},{112,116}} | collective-permute-start | bytes 393224 | tf_op jit(solution)/shard_map/ppermute | solution.py:29
  60.9 13.4 %collective-permute-start.4 = (bf16[128,512]{0,1:T(8,128)(2,1)}, bf16[128,512]{0,1:T(8,128)(2,1)}, u32[]{:S(2)}, u32[]{:S(2)}) collective-permute-start(bf16[128,512]{0,1:T(8,128)(2,1)} %get-tuple-element.38), channel_id=1, source_target_pairs={{0,5},{16,21},{32,37},{48,53},{64,69},{80,85},{96,101},{112,117}} | collective-permute-start | bytes 393224 | tf_op jit(solution)/shard_map/ppermute | solution.py:29
  65.6 12.1 %collective-permute-start.5 = (bf16[128,512]{0,1:T(8,128)(2,1)}, bf16[128,512]{0,1:T(8,128)(2,1)S(1)}, u32[]{:S(2)}, u32[]{:S(2)}) collective-permute-start(bf16[128,512]{0,1:T(8,128)(2,1)} %get-tuple-element.37), channel_id=1, source_target_pairs={{0,6},{16,22},{32,38},{48,54},{64,70},{80,86},{96,102},{112,118}} | collective-permute-start | bytes 393224 | tf_op jit(solution)/shard_map/ppermute | solution.py:29
  66.5 12.6 %collective-permute-start.6 = (bf16[128,512]{0,1:T(8,128)(2,1)}, bf16[128,512]{0,1:T(8,128)(2,1)S(1)}, u32[]{:S(2)}, u32[]{:S(2)}) collective-permute-start(bf16[128,512]{0,1:T(8,128)(2,1)} %get-tuple-element.36), channel_id=1, source_target_pairs={{0,7},{16,23},{32,39},{48,55},{64,71},{80,87},{96,103},{112,119}} | collective-permute-start | bytes 393224 | tf_op jit(solution)/shard_map/ppermute | solution.py:29
  73.7 8.1 %collective-permute-start.8 = (bf16[128,512]{0,1:T(8,128)(2,1)}, bf16[128,512]{0,1:T(8,128)(2,1)S(1)}, u32[]{:S(2)}, u32[]{:S(2)}) collective-permute-start(bf16[128,512]{0,1:T(8,128)(2,1)} %get-tuple-element.34), channel_id=1, source_target_pairs={{0,9},{16,25},{32,41},{48,57},{64,73},{80,89},{96,105},{112,121}} | collective-permute-start | bytes 393224 | tf_op jit(solution)/shard_map/ppermute | solution.py:29
  74.3 8.1 %collective-permute-start.9 = (bf16[128,512]{0,1:T(8,128)(2,1)}, bf16[128,512]{0,1:T(8,128)(2,1)S(1)}, u32[]{:S(2)}, u32[]{:S(2)}) collective-permute-start(bf16[128,512]{0,1:T(8,128)(2,1)} %get-tuple-element.33), channel_id=1, source_target_pairs={{0,10},{16,26},{32,42},{48,58},{64,74},{80,90},{96,106},{112,122}} | collective-permute-start | bytes 393224 | tf_op jit(solution)/shard_map/ppermute | solution.py:29
  80.4 14.2 %collective-permute-start.25 = (bf16[160,512]{0,1:T(8,128)(2,1)S(1)}, bf16[160,512]{0,1:T(8,128)(2,1)S(1)}, u32[]{:S(2)}, u32[]{:S(2)}) collective-permute-start(bf16[160,512]{0,1:T(8,128)(2,1)S(1)} %get-tuple-element.12), channel_id=1, source_target_pairs={{0,3},{16,19},{32,35},{48,51},{64,67},{80,83},{96,99},{112,115}} | collective-permute-start | bytes 491528 | tf_op jit(solution)/shard_map/ppermute | solution.py:29
  81.8 14.3 %collective-permute-start.26 = (bf16[160,512]{0,1:T(8,128)(2,1)S(1)}, bf16[160,512]{0,1:T(8,128)(2,1)S(1)}, u32[]{:S(2)}, u32[]{:S(2)}) collective-permute-start(bf16[160,512]{0,1:T(8,128)(2,1)S(1)} %get-tuple-element.13), channel_id=1, source_target_pairs={{0,4},{16,20},{32,36},{48,52},{64,68},{80,84},{96,100},{112,116}} | collective-permute-start | bytes 491528 | tf_op jit(solution)/shard_map/ppermute | solution.py:29
  82.5 14.9 %collective-permute-start.27 = (bf16[160,512]{0,1:T(8,128)(2,1)S(1)}, bf16[160,512]{0,1:T(8,128)(2,1)S(1)}, u32[]{:S(2)}, u32[]{:S(2)}) collective-permute-start(bf16[160,512]{0,1:T(8,128)(2,1)S(1)} %get-tuple-element.14), channel_id=1, source_target_pairs={{0,5},{16,21},{32,37},{48,53},{64,69},{80,85},{96,101},{112,117}} | collective-permute-start | bytes 491528 | tf_op jit(solution)/shard_map/ppermute | solution.py:29
  84.5 14.4 %collective-permute-start.28 = (bf16[160,512]{0,1:T(8,128)(2,1)}, bf16[160,512]{0,1:T(8,128)(2,1)}, u32[]{:S(2)}, u32[]{:S(2)}) collective-permute-start(bf16[160,512]{0,1:T(8,128)(2,1)} %get-tuple-element.15), channel_id=1, source_target_pairs={{0,6},{16,22},{32,38},{48,54},{64,70},{80,86},{96,102},{112,118}} | collective-permute-start | bytes 491528 | tf_op jit(solution)/shard_map/ppermute | solution.py:29
  85.8 13.7 %collective-permute-start.29 = (bf16[160,512]{0,1:T(8,128)(2,1)}, bf16[160,512]{0,1:T(8,128)(2,1)}, u32[]{:S(2)}, u32[]{:S(2)}) collective-permute-start(bf16[160,512]{0,1:T(8,128)(2,1)} %get-tuple-element.16), channel_id=1, source_target_pairs={{0,7},{16,23},{32,39},{48,55},{64,71},{80,87},{96,103},{112,119}} | collective-permute-start | bytes 491528 | tf_op jit(solution)/shard_map/ppermute | solution.py:29
  109.9 28.9 %collective-permute-start.44 = (bf16[512,1024]{1,0:T(8,128)(2,1)S(1)}, bf16[512,1024]{1,0:T(8,128)(2,1)S(1)}, u32[]{:S(2)}, u32[]{:S(2)}) collective-permute-start(bf16[512,1024]{1,0:T(8,128)(2,1)S(1)} %slice.202), channel_id=1, source_target_pairs={{0,64},{1,65},{2,66},{3,67},{4,68},{5,69},{6,70},{7,71},{8,72},{9,... | collective-permute-start | bytes 3145736 | tf_op jit(solution)/shard_map/ppermute | solution.py:19
  143.3 23.2 %collective-permute-start.40 = (bf16[512,1024]{1,0:T(8,128)(2,1)S(1)}, bf16[512,1024]{1,0:T(8,128)(2,1)S(1)}, u32[]{:S(2)}, u32[]{:S(2)}) collective-permute-start(bf16[512,1024]{1,0:T(8,128)(2,1)S(1)} %get-tuple-element.9), channel_id=1, source_target_pairs={{0,64},{1,65},{2,66},{3,67},{4,68},{5,69},{6,70},{7,71},{8,72},{9,... | collective-permute-start | bytes 3145736 | tf_op jit(solution)/shard_map/ppermute | solution.py:19
  169.3 18.6 %collective-permute-start.45 = (bf16[512,1024]{1,0:T(8,128)(2,1)}, bf16[512,1024]{1,0:T(8,128)(2,1)}, u32[]{:S(2)}, u32[]{:S(2)}) collective-permute-start(bf16[512,1024]{1,0:T(8,128)(2,1)} %get-tuple-element.8), channel_id=1, source_target_pairs={{0,16},{32,48},{64,80},{96,112},{1,17},{33,49},{65,81},{97,113},{2... | collective-permute-start | bytes 3145736 | tf_op jit(solution)/shard_map/ppermute | solution.py:21
  227.8 11.4 %collective-permute-start.46 = (f32[64,128]{1,0:T(8,128)S(1)}, f32[64,128]{1,0:T(8,128)S(1)}, u32[]{:S(2)}, u32[]{:S(2)}) collective-permute-start(f32[64,128]{1,0:T(8,128)S(1)} %reduce_sum.18), channel_id=1, source_target_pairs={{0,16},{16,32},{32,48},{48,64},{64,80},{80,96},{96,112},{1,17},{17... | collective-permute-start | bytes 98312 | tf_op jit(solution)/shard_map/ppermute | solution.py:123
  229.7 9.5 %collective-permute-start.47 = (f32[64,128]{1,0:T(8,128)S(1)}, f32[64,128]{1,0:T(8,128)S(1)}, u32[]{:S(2)}, u32[]{:S(2)}) collective-permute-start(f32[64,128]{1,0:T(8,128)S(1)} %reduce_sum.18), channel_id=1, source_target_pairs={{16,0},{32,16},{48,32},{64,48},{80,64},{96,80},{112,96},{17,1},{33... | collective-permute-start | bytes 98312 | tf_op jit(solution)/shard_map/ppermute | solution.py:124
  236.8 7.9 %collective-permute-start.49 = (f32[64,128]{1,0:T(8,128)S(1)}, f32[64,128]{1,0:T(8,128)S(1)}, u32[]{:S(2)}, u32[]{:S(2)}) collective-permute-start(f32[64,128]{1,0:T(8,128)S(1)} %reduce_sum.18), channel_id=1, source_target_pairs={{1,0},{2,1},{3,2},{4,3},{5,4},{6,5},{7,6},{8,7},{9,8},{10,9},{11,1... | collective-permute-start | bytes 98312 | tf_op jit(solution)/shard_map/ppermute | solution.py:126
  (38 other events, 433.1 us)
Sparse Core Ops, SparseCore 0:
  107.3 79.3 all-gather.2

commit v2 on v0

v2 whole, which is shorter than its diff:
```python
import jax
import jax.numpy as jnp
from jax import lax
from jax.experimental import pallas as pl
from jax.experimental.pallas import tpu as pltpu
from jax.sharding import PartitionSpec as P

BF16 = jnp.bfloat16
F32 = jnp.float32


def multiply(left, right):
    return jnp.dot(left, right, preferred_element_type=F32)


def send(value, axis, pairs):
    return lax.ppermute(value, axis, pairs)


def along_x(value):
    return [send(value, "row", [(0, at)]) for at in (4, 2, 6)]


def on_even(value, got, row):
    return jnp.where(row == 0, value, got[0] + got[1] + got[2])


def gather_first_half(value, col):
    for bit in (1, 2, 4):
        other = send(value, "col", [(at, at ^ bit) for at in range(16)])
        after = (col & bit) == 0
        value = jnp.concatenate(
            [jnp.where(after, value, other), jnp.where(after, other, value)], axis=0
        )
    return jnp.where(col < 8, value, send(value, "col", [(at, at + 8) for at in range(8)]))


def hop_near(value):
    return send(value, "row", [(0, 2)]) + send(value, "row", [(0, 6)])


def hop_far(value, near, row):
    half = value.shape[0] // 2
    far = [send(near[:half], "row", [(2, 4)]), send(near[half:], "row", [(6, 4)])]
    return jnp.where(row == 0, value, near + jnp.concatenate(far, axis=0))


def to_odd(value):
    return send(value, "row", [(at, at + 1) for at in range(0, 8, 2)])


REGIONS = ((1, 5, 13, 2), (3, 7, 15, 0), (4, 8, 6, 9), (12, 14, 11, 10))


def lift_kernel(table_ref, *refs):
    tiles, (mixed_ref, inverses_ref), outs = refs[:4], refs[4:6], refs[6:]
    panel = inverses_ref.shape[1]
    rows = jnp.concatenate([tile_ref[...] for tile_ref in tiles], axis=0)
    first, second = inverses_ref[0], inverses_ref[1]
    cross = multiply(mixed_ref[:panel], first).astype(BF16)
    low0 = multiply(rows[:, :panel], first).astype(BF16)
    low1 = rows[:, panel:].astype(F32) - multiply(low0, mixed_ref[panel:])
    low1 = multiply(low1.astype(BF16), second).astype(BF16)
    low0 = (low0.astype(F32) - multiply(low1, cross)).astype(BF16)
    done = jnp.concatenate([low0, low1], axis=1)
    for which, out_ref in enumerate(outs):

        @pl.when(pl.program_id(0) == which)
        def _(out_ref=out_ref):
            out_ref[...] = done


def lift(panels, mixed, inverses, tile):
    depth = inverses.shape[0] * inverses.shape[1]
    table = jnp.array([at for members in REGIONS for at in members], dtype=jnp.int32)
    bundle = jax.ShapeDtypeStruct((4 * tile, depth), BF16)
    return pl.pallas_call(
        lift_kernel,
        grid_spec=pltpu.PrefetchScalarGridSpec(
            num_scalar_prefetch=1,
            grid=(4,),
            in_specs=[
                pl.BlockSpec((tile, depth), lambda i, table, j=j: (table[4 * i + j], 0))
                for j in range(4)
            ]
            + [
                pl.BlockSpec(mixed.shape, lambda i, table: (0, 0)),
                pl.BlockSpec(inverses.shape, lambda i, table: (0, 0, 0)),
            ],
            out_specs=[pl.BlockSpec(bundle.shape, lambda i, table: (0, 0)) for _ in REGIONS],
        ),
        out_shape=[bundle] * 4,
        compiler_params=pltpu.CompilerParams(vmem_limit_bytes=40 << 20),
    )(table, *([panels] * 4), mixed, inverses)


def pass_on(bundles, col, tile):
    own = bundles[1][3 * tile :]
    got = [send(bundle, "col", [(0, members[0])]) for bundle, members in zip(bundles, REGIONS)]
    got = got[0] + got[1] + got[2] + got[3]
    piece = jnp.where(col == 0, own, got[:tile])
    for j in range(1, 4):
        part = got[j * tile : (j + 1) * tile]
        piece = piece + send(part, "col", [(m[0], m[j]) for m in REGIONS if m[j] != 0])
    return piece


def adjoint_kernel(raw_ref, parts_ref, piece_ref, out_ref):
    sources, tile = raw_ref.shape
    total = raw_ref[...]
    for k in range(parts_ref.shape[0] // sources):
        total = total - lax.dot_general(
            parts_ref[k * sources : (k + 1) * sources],
            piece_ref[:, k * tile : (k + 1) * tile].astype(F32),
            (((1,), (1,)), ((), ())),
            precision=lax.Precision.HIGHEST,
            preferred_element_type=F32,
        )
    out_ref[...] = total


def update_kernel(base_ref, low_ref, mixed_ref, plain_ref, out_ref, up_ref):
    rows, width = base_ref.shape
    half = up_ref.shape[0] // 2

    @pl.when(pl.program_id(0) == 0)
    def _():
        up_ref[:half, :half] = plain_ref[:half]
        up_ref[:half, half:] = mixed_ref[half:]
        up_ref[half:, :half] = mixed_ref[:half]
        up_ref[half:, half:] = plain_ref[half:]

    low = low_ref[...].reshape(rows, up_ref.shape[0])
    out_ref[...] = (base_ref[...].astype(F32) - multiply(low, up_ref[...])).astype(BF16)


def update(base, low, mixed, plain):
    rows, width = base.shape
    tiles, tile, depth = low.shape
    group = 4
    step = group * tile
    return pl.pallas_call(
        update_kernel,
        grid=(rows // step,),
        in_specs=[
            pl.BlockSpec((step, width), lambda i: (i, 0)),
            pl.BlockSpec((group, tile, depth), lambda i: (i, 0, 0)),
            pl.BlockSpec(mixed.shape, lambda i: (0, 0)),
            pl.BlockSpec(plain.shape, lambda i: (0, 0)),
        ],
        out_specs=pl.BlockSpec((step, width), lambda i: (i, 0)),
        out_shape=jax.ShapeDtypeStruct((rows, width), BF16),
        scratch_shapes=[pltpu.VMEM((depth, width), BF16)],
        compiler_params=pltpu.CompilerParams(vmem_limit_bytes=56 << 20),
    )(base, low, mixed, plain)


def shards(matrix, inverses, adjoint, focal_nodes, adjacency, conductance):
    row, col = lax.axis_index("row"), lax.axis_index("col")
    rows_axis, cols = lax.axis_size("row"), lax.axis_size("col")
    panel = inverses.shape[1]
    both = 2 * panel
    sources = adjoint.shape[0]
    rows_here, width_here = matrix.shape
    tile = rows_here // cols
    even = row % 2 == 0

    mixed = jnp.concatenate([matrix[panel:both, :panel], matrix[:panel, panel:both]], axis=0)
    upper_half = lax.broadcasted_iota(jnp.int32, (both, panel), 0) < panel
    plain = jnp.where(upper_half, matrix[:both, :panel], matrix[:both, panel:both])

    mixed = hop_far(mixed, hop_near(mixed), row)
    mixed = jnp.where(even, mixed, to_odd(mixed))
    positions = col * width_here + lax.broadcasted_iota(jnp.int32, (sources, width_here), 1)
    onehot = (positions == focal_nodes[:, None]).astype(BF16)
    stacked = jnp.concatenate([adjoint, onehot], axis=0)
    product = lax.dot_general(
        stacked, matrix, (((1,), (1,)), ((), ())), preferred_element_type=F32
    )
    raw = product[:sources] + product[sources:]
    mixed, raw, plain = lax.optimization_barrier((mixed, raw, plain))

    bundles = lift(matrix, mixed, inverses, tile)
    bundles, raw = lax.optimization_barrier((bundles, raw))
    swapped = lax.all_to_all(
        raw.reshape(sources, cols, tile), "col", split_axis=1, concat_axis=0, tiled=True
    )
    raw_tile = jnp.sum(swapped.reshape(cols, sources, tile), axis=0)
    piece = pass_on(bundles, col, tile)
    piece, raw_tile, plain = lax.optimization_barrier((piece, raw_tile, plain))
    low = lax.all_gather(piece, "col")
    parts = gather_first_half(raw_tile, col)

    parts = on_even(parts, along_x(parts), row)
    parts = jnp.where(even, parts, to_odd(parts))
    plain = on_even(plain, along_x(plain), row)
    plain = jnp.where(even, plain, to_odd(plain))
    parts, plain = lax.optimization_barrier((parts, plain))
    trailing = update(matrix, low, mixed, plain)
    injected = pl.pallas_call(
        adjoint_kernel, out_shape=jax.ShapeDtypeStruct((sources, tile), F32)
    )(raw_tile, parts, piece)

    neighbours = (
        [
            send(injected, "row", [(i, i + 1) for i in range(rows_axis - 1)]),
            send(injected, "row", [(i + 1, i) for i in range(rows_axis - 1)]),
            send(injected, "col", [(i, i + 1) for i in range(cols - 1)]),
            send(injected, "col", [(i + 1, i) for i in range(cols - 1)]),
        ]
    )
    neighbours, trailing = lax.optimization_barrier((neighbours, trailing))
    neighbours = jnp.stack(neighbours)
    node_ids = lax.broadcasted_iota(jnp.int32, (1, 1, tile), 2)
    selector = (adjacency[:, :, None] == node_ids).astype(F32)
    gathered = jnp.einsum("ksj,kij->ksi", neighbours, selector, precision=lax.Precision.HIGHEST)
    currents = injected - jnp.sum(conductance[:, None, :] * gathered, axis=0)
    return (trailing, currents)


def solution(mesh):
    placed = (
        P("row", "col"),
        P(),
        P(None, "col"),
        P(),
        P(None, ("row", "col")),
        P(None, ("row", "col")),
    )
    return jax.shard_map(
        shards,
        mesh=mesh,
        in_specs=placed,
        out_specs=(P("row", "col"), P(None, ("row", "col"))),
        check_vma=False,
    )
```

time: 451 us -> 186 us (0.41)
  waiting for transfers between devices: 388 us -> 71.1 us
  starting transfers between devices: 12.2 us -> 57.8 us
  Pallas kernels: 0 us -> 20.5 us
  matrix products: 21.4 us -> 1.96 us
  local copies, waits for them, and re-layouts: 0.03 us -> 4.71 us
    psum x4 -> x0, waiting for transfers between devices: 307 us -> none  [spread(): return lax.psum(kept, axis)]
    reduce_scatter x1 -> x0, waiting for transfers between devices: 71.9 us -> none  [shards(): lax.psum_scatter(partial_sum, 'col', scatter_dimension=1, tiled=True)]
    ppermute x4 -> x28, waiting for transfers between devices: 9.4 us -> 71.1 us  [send(): return lax.ppermute(value, axis, pairs)]
    ppermute x4 -> x28, starting transfers between devices: 12 us -> 46.1 us  [send(): return lax.ppermute(value, axis, pairs)]
    pallas_call x0 -> x3, Pallas kernels: none -> 20.5 us  [the longest x1 9.21 us: update(): pl.pallas_call(update_kernel, grid=(rows // step,), in_specs=[pl.BlockSpe...]
    dot_general x3 -> x1, matrix products: 20.9 us -> 1.53 us  [shards(): lax.dot_general(stacked, matrix, (((1,), (1,)), ((), ())), preferred_elem...]
    all_to_all x0 -> x1, starting transfers between devices: none -> 11.6 us  [shards(): lax.all_to_all(raw.reshape(sources, cols, tile), 'col', split_axis=1, con...]
    select_n x4 -> x11, other arithmetic: 10.8 us -> 6.68 us  [the longest x1 2.73 us: shards(): jnp.where(upper_half, matrix[:both, :panel], matrix[:both, panel:both])]
  transfers between devices with their start and end apart: 9 -> 30, of which waited for: 8 -> 12; matrix products, arithmetic and copies ran while one was open for 1% -> 7% of each run, Pallas kernels for 0% -> 7%
where the time goes in v2:
time: 186 us; the launch traced here: 185 us
  waiting for transfers between devices  71.1 us (38%)
  starting transfers between devices  57.8 us (31%)
  Pallas kernels  20.5 us (11%)
  between operations  14.6 us (8%)
  other arithmetic  13.9 us (7%)
  local copies, waits for them, and re-layouts  4.71 us (3%)
  matrix products  1.96 us (1%)
    ppermute x28, waiting for transfers between devices, send(): return lax.ppermute(value, axis, pairs)  71.1 us
    ppermute x28, starting transfers between devices, send(): return lax.ppermute(value, axis, pairs)  46.1 us
    all_to_all x1, starting transfers between devices, shards(): lax.all_to_all(raw.reshape(sources, cols, tile), 'col', split_axis=1, con...  11.6 us
    pallas_call x1, Pallas kernels, update(): pl.pallas_call(update_kernel, grid=(rows // step,), in_specs=[pl.BlockSpe...  9.21 us
    pallas_call x1, Pallas kernels, lift(): pl.pallas_call(lift_kernel, grid_spec=pltpu.PrefetchScalarGridSpec(num_sc...  8.45 us
  transfers between devices with their start and end apart: 30, of which 12 were waited for; matrix products, arithmetic and copies ran while one was open for 7% of the time, Pallas kernels for 7%

profile of v2, /device:TPU:34, one launch (start us, length us, event | category | flops | bytes accessed | tf_op | source)
XLA Modules:
  0.0 184.5 jit_solution(10122799670898029294)
XLA Ops:
  10.6 14.7 %collective-permute-done = bf16[1024,512]{1,0:T(8,128)(2,1)S(1)} collective-permute-done((bf16[1024,512]{1,0:T(8,128)(2,1)S(1)}, bf16[1024,512]{1,0:T(8,128)(2,1)S(1)}, u32[]{:S(2)}, u32[]{:S(2)}) %collective-permute-start) | collective-permute-done | bytes 1048608 | tf_op jit(solution)/shard_map/ppermute | solution.py:17
  27.3 1.3 collective-permute-start.2
  28.7 2.7 %slice_select_fusion = bf16[1024,512]{1,0:T(8,128)(2,1)} fusion(bf16[2048,1024]{1,0:T(8,128)(2,1)} %base_ref.1, pred[1024]{0:T(1024)(128)(4,1)S(1)} %iota_compare_fusion.2), kind=kLoop, calls=%fused_computation.7 | loop fusion | flops 524288 | bytes 3146752 | tf_op jit(solution)/shard_map/jit(_where)/select_n | solution.py:170
  31.4 4.2 %collective-permute-done.2 = bf16[512,512]{1,0:T(8,128)(2,1)S(1)} collective-permute-done((bf16[512,512]{1,0:T(8,128)(2,1)}, bf16[512,512]{1,0:T(8,128)(2,1)S(1)}, u32[]{:S(2)}, u32[]{:S(2)}) %collective-permute-start.2) | collective-permute-done | bytes 524320 | tf_op jit(solution)/shard_map/ppermute | solution.py:17
  36.0 1.4 collective-permute-start.4
  37.5 1.5 fusion.5
  40.2 8.4 %shard_map.86 = (bf16[512,1024]{1,0:T(8,128)(2,1)S(1)}, bf16[512,1024]{1,0:T(8,128)(2,1)S(1)}, bf16[512,1024]{1,0:T(8,128)(2,1)}, bf16[512,1024]{1,0:T(8,128)(2,1)}) custom-call(s32[16]{0:T(128)S(1)} %copy-done.3, bf16[2048,1024]{1,0:T(8,128)(2,1)S(1)} %copy-done, bf16[2048,1024]{1,0:T(8,128)(2,1)S(1)} %copy-done, bf16[2048,1024]{1,0:T(8,128)(2,1)S(1)} %copy-done, ...), custom_call_target="tpu_custom_call" | custom-call | tf_op jit(solution)/shard_map/pallas_call | solution.py:77
  50.7 1.6 collective-permute-start.5
  52.4 1.6 collective-permute-start.6
  54.9 11.6 %all-to-all-start = ((f32[64,16,128]{2,0,1:T(8,128)}), f32[64,16,128]{2,0,1:T(8,128)}, u32[]{:S(2)}, u32[]{:S(2)}) async-start(f32[64,16,128]{2,0,1:T(8,128)} %copy_bitcast_fusion), calls=%async_computation | async-start | bytes 1048576 | tf_op jit(solution)/shard_map/all_to_all | solution.py:185
  66.6 17.6 %collective-permute-done.7 = bf16[512,1024]{1,0:T(8,128)(2,1)} collective-permute-done((bf16[512,1024]{1,0:T(8,128)(2,1)}, bf16[512,1024]{1,0:T(8,128)(2,1)}, u32[]{:S(2)}, u32[]{:S(2)}) %collective-permute-start.7) | collective-permute-done | bytes 1048608 | tf_op jit(solution)/shard_map/ppermute | solution.py:17
  84.2 2.4 %add_add_fusion = bf16[512,1024]{1,0:T(8,128)(2,1)S(1)} fusion(bf16[512,1024]{1,0:T(8,128)(2,1)} %copy-done.5, bf16[512,1024]{1,0:T(8,128)(2,1)} %collective-permute-done.7, bf16[512,1024]{1,0:T(8,128)(2,1)} %collective-permute-done.5, bf16[512,1024]{1,0:T(8,128)(2,1)} %collective-permute-done.6), kind=kLoop, calls=%fused_computation.6 | loop fusion | flops 1572864 | bytes 5242880 | tf_op jit(solution)/shard_map/add | solution.py:100
  87.5 2.0 %collective-permute-start.11 = (bf16[128,1024]{1,0:T(8,128)(2,1)}, bf16[128,1024]{1,0:T(8,128)(2,1)}, u32[]{:S(2)}, u32[]{:S(2)}) collective-permute-start(bf16[128,1024]{1,0:T(8,128)(2,1)} %get-tuple-element.49), channel_id=1, source_target_pairs={{1,2},{4,9},{12,10},{17,18},{20,25},{28,26},{33,34},{36,41},{44,42... | collective-permute-start | bytes 786440 | tf_op jit(solution)/shard_map/ppermute | solution.py:17
  89.5 2.0 %collective-permute-start.10 = (bf16[128,1024]{1,0:T(8,128)(2,1)}, bf16[128,1024]{1,0:T(8,128)(2,1)}, u32[]{:S(2)}, u32[]{:S(2)}) collective-permute-start(bf16[128,1024]{1,0:T(8,128)(2,1)} %get-tuple-element.50), channel_id=1, source_target_pairs={{1,13},{3,15},{4,6},{12,11},{17,29},{19,31},{20,22},{28,27},{33,45... | collective-permute-start | bytes 786440 | tf_op jit(solution)/shard_map/ppermute | solution.py:17
  91.5 2.0 %collective-permute-start.9 = (bf16[128,1024]{1,0:T(8,128)(2,1)}, bf16[128,1024]{1,0:T(8,128)(2,1)}, u32[]{:S(2)}, u32[]{:S(2)}) collective-permute-start(bf16[128,1024]{1,0:T(8,128)(2,1)} %get-tuple-element.48), channel_id=1, source_target_pairs={{1,5},{3,7},{4,8},{12,14},{17,21},{19,23},{20,24},{28,30},{33,37},... | collective-permute-start | bytes 786440 | tf_op jit(solution)/shard_map/ppermute | solution.py:17
  95.8 3.1 %collective-permute-done.10 = bf16[128,1024]{1,0:T(8,128)(2,1)} collective-permute-done((bf16[128,1024]{1,0:T(8,128)(2,1)}, bf16[128,1024]{1,0:T(8,128)(2,1)}, u32[]{:S(2)}, u32[]{:S(2)}) %collective-permute-start.10) | collective-permute-done | bytes 262176 | tf_op jit(solution)/shard_map/ppermute | solution.py:17
  99.0 1.9 %fusion.4.piece_ref = bf16[128,1024]{1,0:T(8,128)(2,1)} fusion(bf16[128,1024]{1,0:T(8,128)(2,1)} %collective-permute-done.11, bf16[128,1024]{1,0:T(8,128)(2,1)} %collective-permute-done.10, bf16[128,1024]{1,0:T(8,128)(2,1)} %collective-permute-done.9, bf16[512,1024]{1,0:T(8,128)(2,1)S(1)} %add_add_fusion, bf16[512,1024]{1,0:T(8,128)(2,1)S(1)} %get-tuple-element.30, ...), kind=kLoop, calls=%fused_computation.15 | loop fusion | flops 524288 | bytes 1572865 | tf_op jit(solution)/shard_map/add | solution.py:104
  104.9 4.9 %collective-permute-start.13 = (f32[128,128]{1,0:T(8,128)S(1)}, f32[128,128]{1,0:T(8,128)S(1)}, u32[]{:S(2)}, u32[]{:S(2)}) collective-permute-start(f32[128,128]{1,0:T(8,128)S(1)} %pad_maximum_fusion.3), channel_id=1, source_target_pairs={{0,2},{1,3},{2,0},{3,1},{4,6},{5,7},{6,4},{7,5},{8,10},{9,11},{10,... | collective-permute-start | bytes 196616 | tf_op jit(solution)/shard_map/ppermute | solution.py:17
  109.8 2.2 %collective-permute-done.13 = f32[128,128]{1,0:T(8,128)S(1)} collective-permute-done((f32[128,128]{1,0:T(8,128)S(1)}, f32[128,128]{1,0:T(8,128)S(1)}, u32[]{:S(2)}, u32[]{:S(2)}) %collective-permute-start.13) | collective-permute-done | bytes 65568 | tf_op jit(solution)/shard_map/ppermute | solution.py:17
  112.7 5.6 %collective-permute-done.14 = f32[256,128]{1,0:T(8,128)S(1)} collective-permute-done((f32[256,128]{1,0:T(8,128)}, f32[256,128]{1,0:T(8,128)S(1)}, u32[]{:S(2)}, u32[]{:S(2)}) %collective-permute-start.14) | collective-permute-done | bytes 131104 | tf_op jit(solution)/shard_map/ppermute | solution.py:17
  118.3 3.0 %collective-permute-start.15 = (f32[512,128]{1,0:T(8,128)S(1)}, f32[512,128]{1,0:T(8,128)S(1)}, u32[]{:S(2)}, u32[]{:S(2)}) collective-permute-start(f32[512,128]{1,0:T(8,128)S(1)} %pad_maximum_fusion.1), channel_id=1, source_target_pairs={{0,8},{1,9},{2,10},{3,11},{4,12},{5,13},{6,14},{7,15},{16,24},{17,... | collective-permute-start | bytes 786440 | tf_op jit(solution)/shard_map/ppermute | solution.py:17
  121.3 12.8 %collective-permute-done.21 = bf16[1024,512]{1,0:T(8,128)(2,1)} collective-permute-done((bf16[1024,512]{1,0:T(8,128)(2,1)S(1)}, bf16[1024,512]{1,0:T(8,128)(2,1)}, u32[]{:S(2)}, u32[]{:S(2)}) %collective-permute-start.21) | collective-permute-done | bytes 1048608 | tf_op jit(solution)/shard_map/ppermute | solution.py:17
  134.1 1.4 add_select_fusion
  135.5 1.4 collective-permute-start.23
  139.6 6.9 %collective-permute-done.17 = f32[512,128]{1,0:T(8,128)S(1)} collective-permute-done((f32[512,128]{1,0:T(8,128)S(1)}, f32[512,128]{1,0:T(8,128)S(1)}, u32[]{:S(2)}, u32[]{:S(2)}) %collective-permute-start.17) | collective-permute-done | bytes 262176 | tf_op jit(solution)/shard_map/ppermute | solution.py:17
  146.6 1.3 collective-permute-start.19
  150.9 2.8 %shard_map.87 = f32[64,128]{1,0:T(8,128)} custom-call(f32[64,128]{1,0:T(8,128)} %copy-done.6, f32[512,128]{1,0:T(8,128)} %broadcast_select_fusion.3.parts_ref, bf16[128,1024]{1,0:T(8,128)(2,1)} %fusion.4.piece_ref), custom_call_target="tpu_custom_call" | custom-call | tf_op jit(solution)/shard_map/pallas_call | solution.py:200
  153.7 2.3 %collective-permute-start.24 = (f32[64,128]{1,0:T(8,128)}, f32[64,128]{1,0:T(8,128)S(1)}, u32[]{:S(2)}, u32[]{:S(2)}) collective-permute-start(f32[64,128]{1,0:T(8,128)} %shard_map.87), channel_id=1, source_target_pairs={{0,16},{16,32},{32,48},{48,64},{64,80},{80,96},{96,112},{1,17},{17... | collective-permute-start | bytes 98312 | tf_op jit(solution)/shard_map/ppermute | solution.py:17
  156.0 3.3 %collective-permute-start.25 = (f32[64,128]{1,0:T(8,128)}, f32[64,128]{1,0:T(8,128)S(1)}, u32[]{:S(2)}, u32[]{:S(2)}) collective-permute-start(f32[64,128]{1,0:T(8,128)} %shard_map.87), channel_id=1, source_target_pairs={{16,0},{32,16},{48,32},{64,48},{80,64},{96,80},{112,96},{17,1},{33... | collective-permute-start | bytes 98312 | tf_op jit(solution)/shard_map/ppermute | solution.py:17
  159.3 3.9 %collective-permute-start.26 = (f32[64,128]{1,0:T(8,128)}, f32[64,128]{1,0:T(8,128)S(1)}, u32[]{:S(2)}, u32[]{:S(2)}) collective-permute-start(f32[64,128]{1,0:T(8,128)} %shard_map.87), channel_id=1, source_target_pairs={{0,1},{1,2},{2,3},{3,4},{4,5},{5,6},{6,7},{7,8},{8,9},{9,10},{10,1... | collective-permute-start | bytes 98312 | tf_op jit(solution)/shard_map/ppermute | solution.py:17
  163.2 4.1 %collective-permute-start.27 = (f32[64,128]{1,0:T(8,128)}, f32[64,128]{1,0:T(8,128)S(1)}, u32[]{:S(2)}, u32[]{:S(2)}) collective-permute-start(f32[64,128]{1,0:T(8,128)} %shard_map.87), channel_id=1, source_target_pairs={{1,0},{2,1},{3,2},{4,3},{5,4},{6,5},{7,6},{8,7},{9,8},{10,9},{11,1... | collective-permute-start | bytes 98312 | tf_op jit(solution)/shard_map/ppermute | solution.py:17
  167.3 9.2 %shard_map.88 = bf16[2048,1024]{1,0:T(8,128)(2,1)} custom-call(bf16[2048,1024]{1,0:T(8,128)(2,1)} %base_ref.1, bf16[16,128,1024]{2,1,0:T(8,128)(2,1)} %bitcast.11, bf16[1024,512]{1,0:T(8,128)(2,1)} %copy-done.1, bf16[1024,512]{1,0:T(8,128)(2,1)} %broadcast_select_fusion.plain_ref), custom_call_target="tpu_custom_call" | custom-call | tf_op jit(solution)/shard_map/pallas_call | solution.py:142
  (86 shorter events, 24.8 us)
Async XLA Ops:
  8.5 16.7 %collective-permute-start = (bf16[1024,512]{1,0:T(8,128)(2,1)S(1)}, bf16[1024,512]{1,0:T(8,128)(2,1)S(1)}, u32[]{:S(2)}, u32[]{:S(2)}) collective-permute-start(bf16[1024,512]{1,0:T(8,128)(2,1)S(1)} %pad_maximum_fusion), channel_id=1, source_target_pairs={{0,32},{1,33},{2,34},{3,35},{4,36},{5,37},{6,38},{7,39},{8,40},{9,... | collective-permute-start | bytes 3145736 | tf_op jit(solution)/shard_map/ppermute | solution.py:17
  9.8 15.4 %collective-permute-start.1 = (bf16[1024,512]{1,0:T(8,128)(2,1)S(1)}, bf16[1024,512]{1,0:T(8,128)(2,1)S(1)}, u32[]{:S(2)}, u32[]{:S(2)}) collective-permute-start(bf16[1024,512]{1,0:T(8,128)(2,1)S(1)} %pad_maximum_fusion), channel_id=1, source_target_pairs={{0,96},{1,97},{2,98},{3,99},{4,100},{5,101},{6,102},{7,103},{8,104... | collective-permute-start | bytes 3145736 | tf_op jit(solution)/shard_map/ppermute | solution.py:17
  26.6 4.8 %collective-permute-start.3 = (bf16[512,512]{1,0:T(8,128)(2,1)}, bf16[512,512]{1,0:T(8,128)(2,1)S(1)}, u32[]{:S(2)}, u32[]{:S(2)}) collective-permute-start(bf16[512,512]{1,0:T(8,128)(2,1)} %get-tuple-element.52), channel_id=1, source_target_pairs={{96,64},{97,65},{98,66},{99,67},{100,68},{101,69},{102,70},{103,71... | collective-permute-start | bytes 1572872 | tf_op jit(solution)/shard_map/ppermute | solution.py:17
  27.3 8.3 %collective-permute-start.2 = (bf16[512,512]{1,0:T(8,128)(2,1)}, bf16[512,512]{1,0:T(8,128)(2,1)S(1)}, u32[]{:S(2)}, u32[]{:S(2)}) collective-permute-start(bf16[512,512]{1,0:T(8,128)(2,1)} %get-tuple-element.51), channel_id=1, source_target_pairs={{32,64},{33,65},{34,66},{35,67},{36,68},{37,69},{38,70},{39,71},{4... | collective-permute-start | bytes 1572872 | tf_op jit(solution)/shard_map/ppermute | solution.py:17
  36.0 3.6 %collective-permute-start.4 = (bf16[1024,512]{1,0:T(8,128)(2,1)S(1)}, bf16[1024,512]{1,0:T(8,128)(2,1)S(1)}, u32[]{:S(2)}, u32[]{:S(2)}) collective-permute-start(bf16[1024,512]{1,0:T(8,128)(2,1)S(1)} %fusion.1), channel_id=1, source_target_pairs={{0,16},{32,48},{64,80},{96,112},{1,17},{33,49},{65,81},{97,113},{2... | collective-permute-start | bytes 3145736 | tf_op jit(solution)/shard_map/ppermute | solution.py:17
  48.7 17.8 %collective-permute-start.8 = (bf16[512,1024]{1,0:T(8,128)(2,1)}, bf16[512,1024]{1,0:T(8,128)(2,1)S(1)}, u32[]{:S(2)}, u32[]{:S(2)}) collective-permute-start(bf16[512,1024]{1,0:T(8,128)(2,1)} %get-tuple-element.33), channel_id=1, source_target_pairs={{0,12},{16,28},{32,44},{48,60},{64,76},{80,92},{96,108},{112,124}} | collective-permute-start | bytes 3145736 | tf_op jit(solution)/shard_map/ppermute | solution.py:17
  49.4 34.8 %collective-permute-start.7 = (bf16[512,1024]{1,0:T(8,128)(2,1)}, bf16[512,1024]{1,0:T(8,128)(2,1)}, u32[]{:S(2)}, u32[]{:S(2)}) collective-permute-start(bf16[512,1024]{1,0:T(8,128)(2,1)} %get-tuple-element.32), channel_id=1, source_target_pairs={{0,4},{16,20},{32,36},{48,52},{64,68},{80,84},{96,100},{112,116}} | collective-permute-start | bytes 3145736 | tf_op jit(solution)/shard_map/ppermute | solution.py:17
  50.7 33.5 %collective-permute-start.5 = (bf16[512,1024]{1,0:T(8,128)(2,1)S(1)}, bf16[512,1024]{1,0:T(8,128)(2,1)}, u32[]{:S(2)}, u32[]{:S(2)}) collective-permute-start(bf16[512,1024]{1,0:T(8,128)(2,1)S(1)} %get-tuple-element.31), channel_id=1, source_target_pairs={{0,1},{16,17},{32,33},{48,49},{64,65},{80,81},{96,97},{112,113}} | collective-permute-start | bytes 3145736 | tf_op jit(solution)/shard_map/ppermute | solution.py:17
  52.4 31.8 %collective-permute-start.6 = (bf16[512,1024]{1,0:T(8,128)(2,1)S(1)}, bf16[512,1024]{1,0:T(8,128)(2,1)}, u32[]{:S(2)}, u32[]{:S(2)}) collective-permute-start(bf16[512,1024]{1,0:T(8,128)(2,1)S(1)} %get-tuple-element.30), channel_id=1, source_target_pairs={{0,3},{16,19},{32,35},{48,51},{64,67},{80,83},{96,99},{112,115}} | collective-permute-start | bytes 3145736 | tf_op jit(solution)/shard_map/ppermute | solution.py:17
  54.9 38.7 %all-to-all-start = ((f32[64,16,128]{2,0,1:T(8,128)}), f32[64,16,128]{2,0,1:T(8,128)}, u32[]{:S(2)}, u32[]{:S(2)}) async-start(f32[64,16,128]{2,0,1:T(8,128)} %copy_bitcast_fusion), calls=%async_computation | async-start | bytes 1048576 | tf_op jit(solution)/shard_map/all_to_all | solution.py:185
  66.5 100.8 %all-gather.3.cloned.1.call-start = ((), (), s32[]{:S(2)}) async-start(), calls=%async_computation.1 | async-start | bytes 4456448 | tf_op jit(solution)/shard_map/all_gather | solution.py:191
  66.6 17.6 %copy-start.5 = (bf16[512,1024]{1,0:T(8,128)(2,1)}, bf16[512,1024]{1,0:T(8,128)(2,1)S(1)}, u32[]{:S(2)}) copy-start(bf16[512,1024]{1,0:T(8,128)(2,1)S(1)} %collective-permute-done.8) | copy-start | bytes 3145732
  87.5 8.3 %collective-permute-start.11 = (bf16[128,1024]{1,0:T(8,128)(2,1)}, bf16[128,1024]{1,0:T(8,128)(2,1)}, u32[]{:S(2)}, u32[]{:S(2)}) collective-permute-start(bf16[128,1024]{1,0:T(8,128)(2,1)} %get-tuple-element.49), channel_id=1, source_target_pairs={{1,2},{4,9},{12,10},{17,18},{20,25},{28,26},{33,34},{36,41},{44,42... | collective-permute-start | bytes 786440 | tf_op jit(solution)/shard_map/ppermute | solution.py:17
  89.5 9.5 %collective-permute-start.10 = (bf16[128,1024]{1,0:T(8,128)(2,1)}, bf16[128,1024]{1,0:T(8,128)(2,1)}, u32[]{:S(2)}, u32[]{:S(2)}) collective-permute-start(bf16[128,1024]{1,0:T(8,128)(2,1)} %get-tuple-element.50), channel_id=1, source_target_pairs={{1,13},{3,15},{4,6},{12,11},{17,29},{19,31},{20,22},{28,27},{33,45... | collective-permute-start | bytes 786440 | tf_op jit(solution)/shard_map/ppermute | solution.py:17
  91.5 7.5 %collective-permute-start.9 = (bf16[128,1024]{1,0:T(8,128)(2,1)}, bf16[128,1024]{1,0:T(8,128)(2,1)}, u32[]{:S(2)}, u32[]{:S(2)}) collective-permute-start(bf16[128,1024]{1,0:T(8,128)(2,1)} %get-tuple-element.48), channel_id=1, source_target_pairs={{1,5},{3,7},{4,8},{12,14},{17,21},{19,23},{20,24},{28,30},{33,37},... | collective-permute-start | bytes 786440 | tf_op jit(solution)/shard_map/ppermute | solution.py:17
  94.6 40.9 %copy-start.6 = (f32[64,128]{1,0:T(8,128)}, f32[64,128]{1,0:T(8,128)S(1)}, u32[]{:S(2)}) copy-start(f32[64,128]{1,0:T(8,128)S(1)} %reduce_sum.18.raw_ref) | copy-start | bytes 98308
  100.9 4.0 %collective-permute-start.12 = (f32[64,128]{1,0:T(8,128)S(1)}, f32[64,128]{1,0:T(8,128)S(1)}, u32[]{:S(2)}, u32[]{:S(2)}) collective-permute-start(f32[64,128]{1,0:T(8,128)S(1)} %reduce_sum.18.raw_ref), channel_id=1, source_target_pairs={{0,1},{1,0},{2,3},{3,2},{4,5},{5,4},{6,7},{7,6},{8,9},{9,8},{10,11... | collective-permute-start | bytes 98312 | tf_op jit(solution)/shard_map/ppermute | solution.py:17
  101.0 20.3 %collective-permute-start.22 = (bf16[1024,512]{1,0:T(8,128)(2,1)S(1)}, bf16[1024,512]{1,0:T(8,128)(2,1)S(1)}, u32[]{:S(2)}, u32[]{:S(2)}) collective-permute-start(bf16[1024,512]{1,0:T(8,128)(2,1)S(1)} %copy-done.4), channel_id=1, source_target_pairs={{0,96},{1,97},{2,98},{3,99},{4,100},{5,101},{6,102},{7,103},{8,104... | collective-permute-start | bytes 3145736 | tf_op jit(solution)/shard_map/ppermute | solution.py:17
  101.7 19.6 %collective-permute-start.20 = (bf16[1024,512]{1,0:T(8,128)(2,1)S(1)}, bf16[1024,512]{1,0:T(8,128)(2,1)S(1)}, u32[]{:S(2)}, u32[]{:S(2)}) collective-permute-start(bf16[1024,512]{1,0:T(8,128)(2,1)S(1)} %copy-done.4), channel_id=1, source_target_pairs={{0,64},{1,65},{2,66},{3,67},{4,68},{5,69},{6,70},{7,71},{8,72},{9,... | collective-permute-start | bytes 3145736 | tf_op jit(solution)/shard_map/ppermute | solution.py:17
  102.5 31.6 %collective-permute-start.21 = (bf16[1024,512]{1,0:T(8,128)(2,1)S(1)}, bf16[1024,512]{1,0:T(8,128)(2,1)}, u32[]{:S(2)}, u32[]{:S(2)}) collective-permute-start(bf16[1024,512]{1,0:T(8,128)(2,1)S(1)} %copy-done.4), channel_id=1, source_target_pairs={{0,32},{1,33},{2,34},{3,35},{4,36},{5,37},{6,38},{7,39},{8,40},{9,... | collective-permute-start | bytes 3145736 | tf_op jit(solution)/shard_map/ppermute | solution.py:17
  104.9 7.1 %collective-permute-start.13 = (f32[128,128]{1,0:T(8,128)S(1)}, f32[128,128]{1,0:T(8,128)S(1)}, u32[]{:S(2)}, u32[]{:S(2)}) collective-permute-start(f32[128,128]{1,0:T(8,128)S(1)} %pad_maximum_fusion.3), channel_id=1, source_target_pairs={{0,2},{1,3},{2,0},{3,1},{4,6},{5,7},{6,4},{7,5},{8,10},{9,11},{10,... | collective-permute-start | bytes 196616 | tf_op jit(solution)/shard_map/ppermute | solution.py:17
  112.7 5.6 %collective-permute-start.14 = (f32[256,128]{1,0:T(8,128)}, f32[256,128]{1,0:T(8,128)S(1)}, u32[]{:S(2)}, u32[]{:S(2)}) collective-permute-start(f32[256,128]{1,0:T(8,128)} %pad_maximum_fusion.2), channel_id=1, source_target_pairs={{0,4},{1,5},{2,6},{3,7},{4,0},{5,1},{6,2},{7,3},{8,12},{9,13},{10,... | collective-permute-start | bytes 393224 | tf_op jit(solution)/shard_map/ppermute | solution.py:17
  118.3 18.5 %collective-permute-start.15 = (f32[512,128]{1,0:T(8,128)S(1)}, f32[512,128]{1,0:T(8,128)S(1)}, u32[]{:S(2)}, u32[]{:S(2)}) collective-permute-start(f32[512,128]{1,0:T(8,128)S(1)} %pad_maximum_fusion.1), channel_id=1, source_target_pairs={{0,8},{1,9},{2,10},{3,11},{4,12},{5,13},{6,14},{7,15},{16,24},{17,... | collective-permute-start | bytes 786440 | tf_op jit(solution)/shard_map/ppermute | solution.py:17
  135.5 14.3 %collective-permute-start.23 = (bf16[1024,512]{1,0:T(8,128)(2,1)S(1)}, bf16[1024,512]{1,0:T(8,128)(2,1)S(1)}, u32[]{:S(2)}, u32[]{:S(2)}) collective-permute-start(bf16[1024,512]{1,0:T(8,128)(2,1)S(1)} %add_select_fusion), channel_id=1, source_target_pairs={{0,16},{32,48},{64,80},{96,112},{1,17},{33,49},{65,81},{97,113},{2... | collective-permute-start | bytes 3145736 | tf_op jit(solution)/shard_map/ppermute | solution.py:17
  136.9 2.7 %collective-permute-start.18 = (f32[512,128]{1,0:T(8,128)S(1)}, f32[512,128]{1,0:T(8,128)S(1)}, u32[]{:S(2)}, u32[]{:S(2)}) collective-permute-start(f32[512,128]{1,0:T(8,128)S(1)} %broadcast_select_fusion.2), channel_id=1, source_target_pairs={{0,96},{1,97},{2,98},{3,99},{4,100},{5,101},{6,102},{7,103},{8,104... | collective-permute-start | bytes 786440 | tf_op jit(solution)/shard_map/ppermute | solution.py:17
  137.6 2.0 %collective-permute-start.16 = (f32[512,128]{1,0:T(8,128)S(1)}, f32[512,128]{1,0:T(8,128)S(1)}, u32[]{:S(2)}, u32[]{:S(2)}) collective-permute-start(f32[512,128]{1,0:T(8,128)S(1)} %broadcast_select_fusion.2), channel_id=1, source_target_pairs={{0,64},{1,65},{2,66},{3,67},{4,68},{5,69},{6,70},{7,71},{8,72},{9,... | collective-permute-start | bytes 786440 | tf_op jit(solution)/shard_map/ppermute | solution.py:17
  138.3 8.3 %collective-permute-start.17 = (f32[512,128]{1,0:T(8,128)S(1)}, f32[512,128]{1,0:T(8,128)S(1)}, u32[]{:S(2)}, u32[]{:S(2)}) collective-permute-start(f32[512,128]{1,0:T(8,128)S(1)} %broadcast_select_fusion.2), channel_id=1, source_target_pairs={{0,32},{1,33},{2,34},{3,35},{4,36},{5,37},{6,38},{7,39},{8,40},{9,... | collective-permute-start | bytes 786440 | tf_op jit(solution)/shard_map/ppermute | solution.py:17
  146.6 2.4 %collective-permute-start.19 = (f32[512,128]{1,0:T(8,128)S(1)}, f32[512,128]{1,0:T(8,128)S(1)}, u32[]{:S(2)}, u32[]{:S(2)}) collective-permute-start(f32[512,128]{1,0:T(8,128)S(1)} %add_select_fusion.1), channel_id=1, source_target_pairs={{0,16},{32,48},{64,80},{96,112},{1,17},{33,49},{65,81},{97,113},{2... | collective-permute-start | bytes 786440 | tf_op jit(solution)/shard_map/ppermute | solution.py:17
  153.7 22.8 %collective-permute-start.24 = (f32[64,128]{1,0:T(8,128)}, f32[64,128]{1,0:T(8,128)S(1)}, u32[]{:S(2)}, u32[]{:S(2)}) collective-permute-start(f32[64,128]{1,0:T(8,128)} %shard_map.87), channel_id=1, source_target_pairs={{0,16},{16,32},{32,48},{48,64},{64,80},{80,96},{96,112},{1,17},{17... | collective-permute-start | bytes 98312 | tf_op jit(solution)/shard_map/ppermute | solution.py:17
  156.0 20.5 %collective-permute-start.25 = (f32[64,128]{1,0:T(8,128)}, f32[64,128]{1,0:T(8,128)S(1)}, u32[]{:S(2)}, u32[]{:S(2)}) collective-permute-start(f32[64,128]{1,0:T(8,128)} %shard_map.87), channel_id=1, source_target_pairs={{16,0},{32,16},{48,32},{64,48},{80,64},{96,80},{112,96},{17,1},{33... | collective-permute-start | bytes 98312 | tf_op jit(solution)/shard_map/ppermute | solution.py:17
  159.3 17.3 %collective-permute-start.26 = (f32[64,128]{1,0:T(8,128)}, f32[64,128]{1,0:T(8,128)S(1)}, u32[]{:S(2)}, u32[]{:S(2)}) collective-permute-start(f32[64,128]{1,0:T(8,128)} %shard_map.87), channel_id=1, source_target_pairs={{0,1},{1,2},{2,3},{3,4},{4,5},{5,6},{6,7},{7,8},{8,9},{9,10},{10,1... | collective-permute-start | bytes 98312 | tf_op jit(solution)/shard_map/ppermute | solution.py:17
  163.2 13.4 %collective-permute-start.27 = (f32[64,128]{1,0:T(8,128)}, f32[64,128]{1,0:T(8,128)S(1)}, u32[]{:S(2)}, u32[]{:S(2)}) collective-permute-start(f32[64,128]{1,0:T(8,128)} %shard_map.87), channel_id=1, source_target_pairs={{1,0},{2,1},{3,2},{4,3},{5,4},{6,5},{7,6},{8,7},{9,8},{10,9},{11,1... | collective-permute-start | bytes 98312 | tf_op jit(solution)/shard_map/ppermute | solution.py:17
  (10 other events, 74.4 us)
Sparse Core Ops, SparseCore 0:
  101.0 58.9 all-gather.2

commit v3 on v2

--- a/solution.py
+++ b/solution.py
@@ -33,16 +33,6 @@
             [jnp.where(after, value, other), jnp.where(after, other, value)], axis=0
         )
     return jnp.where(col < 8, value, send(value, "col", [(at, at + 8) for at in range(8)]))
-
-
-def hop_near(value):
-    return send(value, "row", [(0, 2)]) + send(value, "row", [(0, 6)])
-
-
-def hop_far(value, near, row):
-    half = value.shape[0] // 2
-    far = [send(near[:half], "row", [(2, 4)]), send(near[half:], "row", [(6, 4)])]
-    return jnp.where(row == 0, value, near + jnp.concatenate(far, axis=0))
 
 
 def to_odd(value):
@@ -169,27 +159,28 @@
     upper_half = lax.broadcasted_iota(jnp.int32, (both, panel), 0) < panel
     plain = jnp.where(upper_half, matrix[:both, :panel], matrix[:both, panel:both])
 
-    mixed = hop_far(mixed, hop_near(mixed), row)
-    mixed = jnp.where(even, mixed, to_odd(mixed))
+    mixed_lines = along_x(mixed)
     positions = col * width_here + lax.broadcasted_iota(jnp.int32, (sources, width_here), 1)
     onehot = (positions == focal_nodes[:, None]).astype(BF16)
     stacked = jnp.concatenate([adjoint, onehot], axis=0)
     product = lax.dot_general(
         stacked, matrix, (((1,), (1,)), ((), ())), preferred_element_type=F32
     )
-    raw = product[:sources] + product[sources:]
-    mixed, raw, plain = lax.optimization_barrier((mixed, raw, plain))
-
-    bundles = lift(matrix, mixed, inverses, tile)
-    bundles, raw = lax.optimization_barrier((bundles, raw))
+    raw = (product[:sources] + product[sources:]).astype(BF16)
     swapped = lax.all_to_all(
         raw.reshape(sources, cols, tile), "col", split_axis=1, concat_axis=0, tiled=True
     )
-    raw_tile = jnp.sum(swapped.reshape(cols, sources, tile), axis=0)
+    raw_tile = jnp.sum(swapped.reshape(cols, sources, tile).astype(F32), axis=0)
+    mixed_lines, raw_tile = lax.optimization_barrier((mixed_lines, raw_tile))
+    mixed = on_even(mixed, mixed_lines, row)
+    mixed = jnp.where(even, mixed, to_odd(mixed))
+
+    bundles = lift(matrix, mixed, inverses, tile)
+    bundles, raw_tile = lax.optimization_barrier((bundles, raw_tile))
+    parts = gather_first_half(raw_tile, col)
     piece = pass_on(bundles, col, tile)
-    piece, raw_tile, plain = lax.optimization_barrier((piece, raw_tile, plain))
+    piece, plain = lax.optimization_barrier((piece, plain))
     low = lax.all_gather(piece, "col")
-    parts = gather_first_half(raw_tile, col)
 
     parts = on_even(parts, along_x(parts), row)
     parts = jnp.where(even, parts, to_odd(parts))

time: 186 us -> 181 us (0.973)
  starting transfers between devices: 57.8 us -> 52.6 us
  other arithmetic: 13.9 us -> 10.8 us
  waiting for transfers between devices: 71.1 us -> 73.5 us
  matrix products: 1.96 us -> 4.14 us
    all_to_all x1, waiting for transfers between devices: 0.01 us -> 7.07 us  [shards(): lax.all_to_all(raw.reshape(sources, cols, tile), 'col', split_axis=1, con...]
    ppermute x28 -> x27, waiting for transfers between devices: 71.1 us -> 66.4 us  [send(): return lax.ppermute(value, axis, pairs)]
    all_to_all x1, starting transfers between devices: 11.6 us -> 8.07 us  [shards(): lax.all_to_all(raw.reshape(sources, cols, tile), 'col', split_axis=1, con...]
    select_n x1, other arithmetic: 2.73 us -> 0.2 us  [shards(): jnp.where(upper_half, matrix[:both, :panel], matrix[:both, panel:both])]
    dot_general x1, matrix products: 1.53 us -> 3.7 us  [shards(): lax.dot_general(stacked, matrix, (((1,), (1,)), ((), ())), preferred_elem...]
    select_n x2 -> x3, other arithmetic: 1.47 us -> 3.57 us  [on_even(): return jnp.where(row == 0, value, got[0] + got[1] + got[2])]
    ppermute x28 -> x27, starting transfers between devices: 46.1 us -> 44.5 us  [send(): return lax.ppermute(value, axis, pairs)]
  transfers between devices with their start and end apart: 30 -> 29, of which waited for: 12 -> 12; matrix products, arithmetic and copies ran while one was open for 7% -> 5% of each run, Pallas kernels for 7% -> 7%
where the time goes in v3:
time: 181 us; the launch traced here: 180 us
  waiting for transfers between devices  73.5 us (41%)
  starting transfers between devices  52.6 us (29%)
  Pallas kernels  20.8 us (11%)
  between operations  14.5 us (8%)
  other arithmetic  10.8 us (6%)
  matrix products  4.14 us (2%)
  local copies, waits for them, and re-layouts  3.6 us (2%)
    ppermute x27, waiting for transfers between devices, send(): return lax.ppermute(value, axis, pairs)  66.4 us
    ppermute x27, starting transfers between devices, send(): return lax.ppermute(value, axis, pairs)  44.5 us
    pallas_call x1, Pallas kernels, update(): pl.pallas_call(update_kernel, grid=(rows // step,), in_specs=[pl.BlockSpe...  9.21 us
    pallas_call x1, Pallas kernels, lift(): pl.pallas_call(lift_kernel, grid_spec=pltpu.PrefetchScalarGridSpec(num_sc...  8.79 us
    all_to_all x1, starting transfers between devices, shards(): lax.all_to_all(raw.reshape(sources, cols, tile), 'col', split_axis=1, con...  8.07 us
    all_to_all x1, waiting for transfers between devices, shards(): lax.all_to_all(raw.reshape(sources, cols, tile), 'col', split_axis=1, con...  7.07 us
    dot_general x1, matrix products, shards(): lax.dot_general(stacked, matrix, (((1,), (1,)), ((), ())), preferred_elem...  3.7 us
  transfers between devices with their start and end apart: 29, of which 12 were waited for; matrix products, arithmetic and copies ran while one was open for 5% of the time, Pallas kernels for 7%

profile of v3, /device:TPU:34, one launch (start us, length us, event | category | flops | bytes accessed | tf_op | source)
XLA Modules:
  0.0 180.0 jit_solution(4294000560643734396)
XLA Ops:
  7.2 1.3 fusion.20
  10.6 1.7 collective-permute-start.2
  12.4 3.7 %fusion.6 = f32[128,2048]{1,0:T(8,128)S(1)} fusion(bf16[2048,1024]{1,0:T(8,128)(2,1)} %base_ref.1, bf16[64,1024]{1,0:T(8,128)(2,1)S(1)} %compare_convert_fusion, bf16[64,1024]{1,0:T(8,128)(2,1)S(1)} %copy-done.6), kind=kOutput, calls=%fused_computation.18 | convolution fusion | flops 537395200 | bytes 5505024 | tf_op jit(solution)/shard_map/dot_general | solution.py:166
  16.9 8.1 %all-to-all-start = ((bf16[64,16,128]{2,0,1:T(8,128)(2,1)}), bf16[64,16,128]{2,0,1:T(8,128)(2,1)S(1)}, u32[]{:S(2)}, u32[]{:S(2)}) async-start(bf16[64,16,128]{2,0,1:T(8,128)(2,1)} %copy_bitcast_fusion), calls=%async_computation | async-start | bytes 524288 | tf_op jit(solution)/shard_map/all_to_all | solution.py:170
  25.0 7.1 %all-to-all-done = bf16[64,16,128]{2,0,1:T(8,128)(2,1)S(1)} async-done(((bf16[64,16,128]{2,0,1:T(8,128)(2,1)}), bf16[64,16,128]{2,0,1:T(8,128)(2,1)S(1)}, u32[]{:S(2)}, u32[]{:S(2)}) %all-to-all-start) | async-done | bytes 262176 | tf_op jit(solution)/shard_map/all_to_all | solution.py:170
  32.1 6.0 %collective-permute-done.1 = bf16[1024,512]{1,0:T(8,128)(2,1)} collective-permute-done((bf16[1024,512]{1,0:T(8,128)(2,1)S(1)}, bf16[1024,512]{1,0:T(8,128)(2,1)}, u32[]{:S(2)}, u32[]{:S(2)}) %collective-permute-start.1) | collective-permute-done | bytes 1048608 | tf_op jit(solution)/shard_map/ppermute | solution.py:17
  38.1 2.1 %add_select_fusion.1 = bf16[1024,512]{1,0:T(8,128)(2,1)S(1)} fusion(bf16[1024,512]{1,0:T(8,128)(2,1)} %collective-permute-done.2, bf16[1024,512]{1,0:T(8,128)(2,1)S(1)} %collective-permute-done, bf16[1024,512]{1,0:T(8,128)(2,1)} %collective-permute-done.1, pred[]{:T(512)S(6)} %eq.44, bf16[512,512]{1,0:T(8,128)(2,1)S(1)} %get-tuple-element.47, ...), kind=kLoop, calls=%fused_computation.6 | loop fusion | flops 5767168 | bytes 5242881 | tf_op jit(solution)/shard_map/jit(_where)/select_n | solution.py:25
  40.3 2.4 %collective-permute-start.3 = (bf16[1024,512]{1,0:T(8,128)(2,1)S(1)}, bf16[1024,512]{1,0:T(8,128)(2,1)}, u32[]{:S(2)}, u32[]{:S(2)}) collective-permute-start(bf16[1024,512]{1,0:T(8,128)(2,1)S(1)} %add_select_fusion.1), channel_id=1, source_target_pairs={{0,16},{32,48},{64,80},{96,112},{1,17},{33,49},{65,81},{97,113},{2... | collective-permute-start | bytes 3145736 | tf_op jit(solution)/shard_map/ppermute | solution.py:17
  42.7 1.4 collective-permute-done.3
  44.2 2.2 %copy-done = bf16[2048,1024]{1,0:T(8,128)(2,1)S(1)} copy-done((bf16[2048,1024]{1,0:T(8,128)(2,1)S(1)}, bf16[2048,1024]{1,0:T(8,128)(2,1)}, u32[]{:S(2)}) %copy-start) | copy-done | bytes 4194328
  46.4 8.8 %shard_map.86 = (bf16[512,1024]{1,0:T(8,128)(2,1)}, bf16[512,1024]{1,0:T(8,128)(2,1)S(1)}, bf16[512,1024]{1,0:T(8,128)(2,1)}, bf16[512,1024]{1,0:T(8,128)(2,1)}) custom-call(s32[16]{0:T(128)S(1)} %copy-done.4, bf16[2048,1024]{1,0:T(8,128)(2,1)S(1)} %copy-done, bf16[2048,1024]{1,0:T(8,128)(2,1)S(1)} %copy-done, bf16[2048,1024]{1,0:T(8,128)(2,1)S(1)} %copy-done, ...), custom_call_target="tpu_custom_call" | custom-call | tf_op jit(solution)/shard_map/pallas_call | solution.py:67
  57.2 1.7 collective-permute-start.12
  58.9 1.6 collective-permute-start.13
  60.6 25.7 %collective-permute-done.14 = bf16[512,1024]{1,0:T(8,128)(2,1)S(1)} collective-permute-done((bf16[512,1024]{1,0:T(8,128)(2,1)}, bf16[512,1024]{1,0:T(8,128)(2,1)S(1)}, u32[]{:S(2)}, u32[]{:S(2)}) %collective-permute-start.14) | collective-permute-done | bytes 1048608 | tf_op jit(solution)/shard_map/ppermute | solution.py:17
  86.3 1.9 %add_add_fusion = bf16[512,1024]{1,0:T(8,128)(2,1)S(1)} fusion(bf16[512,1024]{1,0:T(8,128)(2,1)S(1)} %collective-permute-done.15, bf16[512,1024]{1,0:T(8,128)(2,1)S(1)} %collective-permute-done.14, bf16[512,1024]{1,0:T(8,128)(2,1)} %collective-permute-done.12, bf16[512,1024]{1,0:T(8,128)(2,1)} %collective-permute-done.13), kind=kLoop, calls=%fused_computation.5 | loop fusion | flops 1572864 | bytes 5242880 | tf_op jit(solution)/shard_map/add | solution.py:90
  90.9 1.3 collective-permute-start.16
  92.4 3.8 %collective-permute-done.18 = bf16[128,1024]{1,0:T(8,128)(2,1)S(1)} collective-permute-done((bf16[128,1024]{1,0:T(8,128)(2,1)S(1)}, bf16[128,1024]{1,0:T(8,128)(2,1)S(1)}, u32[]{:S(2)}, u32[]{:S(2)}) %collective-permute-start.18) | collective-permute-done | bytes 262176 | tf_op jit(solution)/shard_map/ppermute | solution.py:17
  96.2 5.3 %collective-permute-done.17 = bf16[128,1024]{1,0:T(8,128)(2,1)S(1)} collective-permute-done((bf16[128,1024]{1,0:T(8,128)(2,1)S(1)}, bf16[128,1024]{1,0:T(8,128)(2,1)S(1)}, u32[]{:S(2)}, u32[]{:S(2)}) %collective-permute-start.17) | collective-permute-done | bytes 262176 | tf_op jit(solution)/shard_map/ppermute | solution.py:17
  106.4 4.1 %collective-permute-start.5 = (f32[128,128]{1,0:T(8,128)S(1)}, f32[128,128]{1,0:T(8,128)S(1)}, u32[]{:S(2)}, u32[]{:S(2)}) collective-permute-start(f32[128,128]{1,0:T(8,128)S(1)} %pad_maximum_fusion.3), channel_id=1, source_target_pairs={{0,2},{1,3},{2,0},{3,1},{4,6},{5,7},{6,4},{7,5},{8,10},{9,11},{10,... | collective-permute-start | bytes 196616 | tf_op jit(solution)/shard_map/ppermute | solution.py:17
  110.4 2.2 %collective-permute-done.5 = f32[128,128]{1,0:T(8,128)S(1)} collective-permute-done((f32[128,128]{1,0:T(8,128)S(1)}, f32[128,128]{1,0:T(8,128)S(1)}, u32[]{:S(2)}, u32[]{:S(2)}) %collective-permute-start.5) | collective-permute-done | bytes 65568 | tf_op jit(solution)/shard_map/ppermute | solution.py:17
  113.3 6.4 %collective-permute-done.6 = f32[256,128]{1,0:T(8,128)S(1)} collective-permute-done((f32[256,128]{1,0:T(8,128)}, f32[256,128]{1,0:T(8,128)S(1)}, u32[]{:S(2)}, u32[]{:S(2)}) %collective-permute-start.6) | collective-permute-done | bytes 131104 | tf_op jit(solution)/shard_map/ppermute | solution.py:17
  119.8 2.5 %collective-permute-start.7 = (f32[512,128]{1,0:T(8,128)S(1)}, f32[512,128]{1,0:T(8,128)S(1)}, u32[]{:S(2)}, u32[]{:S(2)}) collective-permute-start(f32[512,128]{1,0:T(8,128)S(1)} %pad_maximum_fusion.1), channel_id=1, source_target_pairs={{0,8},{1,9},{2,10},{3,11},{4,12},{5,13},{6,14},{7,15},{16,24},{17,... | collective-permute-start | bytes 786440 | tf_op jit(solution)/shard_map/ppermute | solution.py:17
  122.4 7.2 %collective-permute-done.20 = bf16[1024,512]{1,0:T(8,128)(2,1)} collective-permute-done((bf16[1024,512]{1,0:T(8,128)(2,1)S(1)}, bf16[1024,512]{1,0:T(8,128)(2,1)}, u32[]{:S(2)}, u32[]{:S(2)}) %collective-permute-start.20) | collective-permute-done | bytes 1048608 | tf_op jit(solution)/shard_map/ppermute | solution.py:17
  129.6 1.4 add_select_fusion
  131.0 1.4 collective-permute-start.22
  135.1 6.9 %collective-permute-done.9 = f32[512,128]{1,0:T(8,128)S(1)} collective-permute-done((f32[512,128]{1,0:T(8,128)S(1)}, f32[512,128]{1,0:T(8,128)S(1)}, u32[]{:S(2)}, u32[]{:S(2)}) %collective-permute-start.9) | collective-permute-done | bytes 262176 | tf_op jit(solution)/shard_map/ppermute | solution.py:17
  146.4 2.8 %shard_map.87 = f32[64,128]{1,0:T(8,128)} custom-call(f32[64,128]{1,0:T(8,128)} %copy-done.5, f32[512,128]{1,0:T(8,128)} %broadcast_select_fusion.3.parts_ref, bf16[128,1024]{1,0:T(8,128)(2,1)} %fusion.5.piece_ref), custom_call_target="tpu_custom_call" | custom-call | tf_op jit(solution)/shard_map/pallas_call | solution.py:191
  149.2 2.2 %collective-permute-start.23 = (f32[64,128]{1,0:T(8,128)}, f32[64,128]{1,0:T(8,128)S(1)}, u32[]{:S(2)}, u32[]{:S(2)}) collective-permute-start(f32[64,128]{1,0:T(8,128)} %shard_map.87), channel_id=1, source_target_pairs={{0,16},{16,32},{32,48},{48,64},{64,80},{80,96},{96,112},{1,17},{17... | collective-permute-start | bytes 98312 | tf_op jit(solution)/shard_map/ppermute | solution.py:17
  151.4 3.3 %collective-permute-start.24 = (f32[64,128]{1,0:T(8,128)}, f32[64,128]{1,0:T(8,128)S(1)}, u32[]{:S(2)}, u32[]{:S(2)}) collective-permute-start(f32[64,128]{1,0:T(8,128)} %shard_map.87), channel_id=1, source_target_pairs={{16,0},{32,16},{48,32},{64,48},{80,64},{96,80},{112,96},{17,1},{33... | collective-permute-start | bytes 98312 | tf_op jit(solution)/shard_map/ppermute | solution.py:17
  154.8 3.0 %collective-permute-start.25 = (f32[64,128]{1,0:T(8,128)}, f32[64,128]{1,0:T(8,128)S(1)}, u32[]{:S(2)}, u32[]{:S(2)}) collective-permute-start(f32[64,128]{1,0:T(8,128)} %shard_map.87), channel_id=1, source_target_pairs={{0,1},{1,2},{2,3},{3,4},{4,5},{5,6},{6,7},{7,8},{8,9},{9,10},{10,1... | collective-permute-start | bytes 98312 | tf_op jit(solution)/shard_map/ppermute | solution.py:17
  157.7 5.0 %collective-permute-start.26 = (f32[64,128]{1,0:T(8,128)}, f32[64,128]{1,0:T(8,128)S(1)}, u32[]{:S(2)}, u32[]{:S(2)}) collective-permute-start(f32[64,128]{1,0:T(8,128)} %shard_map.87), channel_id=1, source_target_pairs={{1,0},{2,1},{3,2},{4,3},{5,4},{6,5},{7,6},{8,7},{9,8},{10,9},{11,1... | collective-permute-start | bytes 98312 | tf_op jit(solution)/shard_map/ppermute | solution.py:17
  162.8 9.2 %shard_map.88 = bf16[2048,1024]{1,0:T(8,128)(2,1)} custom-call(bf16[2048,1024]{1,0:T(8,128)(2,1)} %base_ref.1, bf16[16,128,1024]{2,1,0:T(8,128)(2,1)} %bitcast.11, bf16[1024,512]{1,0:T(8,128)(2,1)} %copy-done.2, bf16[1024,512]{1,0:T(8,128)(2,1)} %broadcast_select_fusion.plain_ref), custom_call_target="tpu_custom_call" | custom-call | tf_op jit(solution)/shard_map/pallas_call | solution.py:132
  (79 shorter events, 21.7 us)
Async XLA Ops:
  8.6 23.5 %collective-permute-start = (bf16[1024,512]{1,0:T(8,128)(2,1)S(1)}, bf16[1024,512]{1,0:T(8,128)(2,1)S(1)}, u32[]{:S(2)}, u32[]{:S(2)}) collective-permute-start(bf16[1024,512]{1,0:T(8,128)(2,1)S(1)} %pad_maximum_fusion), channel_id=1, source_target_pairs={{0,64},{1,65},{2,66},{3,67},{4,68},{5,69},{6,70},{7,71},{8,72},{9,... | collective-permute-start | bytes 3145736 | tf_op jit(solution)/shard_map/ppermute | solution.py:17
  9.3 28.8 %collective-permute-start.1 = (bf16[1024,512]{1,0:T(8,128)(2,1)S(1)}, bf16[1024,512]{1,0:T(8,128)(2,1)}, u32[]{:S(2)}, u32[]{:S(2)}) collective-permute-start(bf16[1024,512]{1,0:T(8,128)(2,1)S(1)} %pad_maximum_fusion), channel_id=1, source_target_pairs={{0,32},{1,33},{2,34},{3,35},{4,36},{5,37},{6,38},{7,39},{8,40},{9,... | collective-permute-start | bytes 3145736 | tf_op jit(solution)/shard_map/ppermute | solution.py:17
  10.6 27.5 %collective-permute-start.2 = (bf16[1024,512]{1,0:T(8,128)(2,1)S(1)}, bf16[1024,512]{1,0:T(8,128)(2,1)}, u32[]{:S(2)}, u32[]{:S(2)}) collective-permute-start(bf16[1024,512]{1,0:T(8,128)(2,1)S(1)} %pad_maximum_fusion), channel_id=1, source_target_pairs={{0,96},{1,97},{2,98},{3,99},{4,100},{5,101},{6,102},{7,103},{8,104... | collective-permute-start | bytes 3145736 | tf_op jit(solution)/shard_map/ppermute | solution.py:17
  16.9 15.2 %all-to-all-start = ((bf16[64,16,128]{2,0,1:T(8,128)(2,1)}), bf16[64,16,128]{2,0,1:T(8,128)(2,1)S(1)}, u32[]{:S(2)}, u32[]{:S(2)}) async-start(bf16[64,16,128]{2,0,1:T(8,128)(2,1)} %copy_bitcast_fusion), calls=%async_computation | async-start | bytes 524288 | tf_op jit(solution)/shard_map/all_to_all | solution.py:170
  24.9 137.8 %all-gather.3.cloned.1.call-start = ((), (), s32[]{:S(2)}) async-start(), calls=%async_computation.1 | async-start | bytes 4456448 | tf_op jit(solution)/shard_map/all_gather | solution.py:183
  32.1 74.2 %copy-start.5 = (f32[64,128]{1,0:T(8,128)}, f32[64,128]{1,0:T(8,128)S(1)}, u32[]{:S(2)}) copy-start(f32[64,128]{1,0:T(8,128)S(1)} %convert_reduce_fusion.raw_ref) | copy-start | bytes 98308
  40.3 3.8 %collective-permute-start.3 = (bf16[1024,512]{1,0:T(8,128)(2,1)S(1)}, bf16[1024,512]{1,0:T(8,128)(2,1)}, u32[]{:S(2)}, u32[]{:S(2)}) collective-permute-start(bf16[1024,512]{1,0:T(8,128)(2,1)S(1)} %add_select_fusion.1), channel_id=1, source_target_pairs={{0,16},{32,48},{64,80},{96,112},{1,17},{33,49},{65,81},{97,113},{2... | collective-permute-start | bytes 3145736 | tf_op jit(solution)/shard_map/ppermute | solution.py:17
  55.2 5.4 %collective-permute-start.15 = (bf16[512,1024]{1,0:T(8,128)(2,1)}, bf16[512,1024]{1,0:T(8,128)(2,1)S(1)}, u32[]{:S(2)}, u32[]{:S(2)}) collective-permute-start(bf16[512,1024]{1,0:T(8,128)(2,1)} %get-tuple-element.36), channel_id=1, source_target_pairs={{0,12},{16,28},{32,44},{48,60},{64,76},{80,92},{96,108},{112,124}} | collective-permute-start | bytes 3145736 | tf_op jit(solution)/shard_map/ppermute | solution.py:17
  55.9 30.3 %collective-permute-start.14 = (bf16[512,1024]{1,0:T(8,128)(2,1)}, bf16[512,1024]{1,0:T(8,128)(2,1)S(1)}, u32[]{:S(2)}, u32[]{:S(2)}) collective-permute-start(bf16[512,1024]{1,0:T(8,128)(2,1)} %get-tuple-element.35), channel_id=1, source_target_pairs={{0,4},{16,20},{32,36},{48,52},{64,68},{80,84},{96,100},{112,116}} | collective-permute-start | bytes 3145736 | tf_op jit(solution)/shard_map/ppermute | solution.py:17
  57.2 29.0 %collective-permute-start.12 = (bf16[512,1024]{1,0:T(8,128)(2,1)}, bf16[512,1024]{1,0:T(8,128)(2,1)}, u32[]{:S(2)}, u32[]{:S(2)}) collective-permute-start(bf16[512,1024]{1,0:T(8,128)(2,1)} %get-tuple-element.34), channel_id=1, source_target_pairs={{0,1},{16,17},{32,33},{48,49},{64,65},{80,81},{96,97},{112,113}} | collective-permute-start | bytes 3145736 | tf_op jit(solution)/shard_map/ppermute | solution.py:17
  58.9 27.4 %collective-permute-start.13 = (bf16[512,1024]{1,0:T(8,128)(2,1)S(1)}, bf16[512,1024]{1,0:T(8,128)(2,1)}, u32[]{:S(2)}, u32[]{:S(2)}) collective-permute-start(bf16[512,1024]{1,0:T(8,128)(2,1)S(1)} %get-tuple-element.33), channel_id=1, source_target_pairs={{0,3},{16,19},{32,35},{48,51},{64,67},{80,83},{96,99},{112,115}} | collective-permute-start | bytes 3145736 | tf_op jit(solution)/shard_map/ppermute | solution.py:17
  88.2 8.0 %collective-permute-start.18 = (bf16[128,1024]{1,0:T(8,128)(2,1)S(1)}, bf16[128,1024]{1,0:T(8,128)(2,1)S(1)}, u32[]{:S(2)}, u32[]{:S(2)}) collective-permute-start(bf16[128,1024]{1,0:T(8,128)(2,1)S(1)} %get-tuple-element.49), channel_id=1, source_target_pairs={{1,2},{4,9},{12,10},{17,18},{20,25},{28,26},{33,34},{36,41},{44,42... | collective-permute-start | bytes 786440 | tf_op jit(solution)/shard_map/ppermute | solution.py:17
  89.5 12.0 %collective-permute-start.17 = (bf16[128,1024]{1,0:T(8,128)(2,1)S(1)}, bf16[128,1024]{1,0:T(8,128)(2,1)S(1)}, u32[]{:S(2)}, u32[]{:S(2)}) collective-permute-start(bf16[128,1024]{1,0:T(8,128)(2,1)S(1)} %get-tuple-element.50), channel_id=1, source_target_pairs={{1,13},{3,15},{4,6},{12,11},{17,29},{19,31},{20,22},{28,27},{33,45... | collective-permute-start | bytes 786440 | tf_op jit(solution)/shard_map/ppermute | solution.py:17
  90.9 10.7 %collective-permute-start.16 = (bf16[128,1024]{1,0:T(8,128)(2,1)S(1)}, bf16[128,1024]{1,0:T(8,128)(2,1)S(1)}, u32[]{:S(2)}, u32[]{:S(2)}) collective-permute-start(bf16[128,1024]{1,0:T(8,128)(2,1)S(1)} %get-tuple-element.48), channel_id=1, source_target_pairs={{1,5},{3,7},{4,8},{12,14},{17,21},{19,23},{20,24},{28,30},{33,37},... | collective-permute-start | bytes 786440 | tf_op jit(solution)/shard_map/ppermute | solution.py:17
  102.3 4.0 %collective-permute-start.4 = (f32[64,128]{1,0:T(8,128)S(1)}, f32[64,128]{1,0:T(8,128)S(1)}, u32[]{:S(2)}, u32[]{:S(2)}) collective-permute-start(f32[64,128]{1,0:T(8,128)S(1)} %convert_reduce_fusion.raw_ref), channel_id=1, source_target_pairs={{0,1},{1,0},{2,3},{3,2},{4,5},{5,4},{6,7},{7,6},{8,9},{9,8},{10,11... | collective-permute-start | bytes 98312 | tf_op jit(solution)/shard_map/ppermute | solution.py:17
  103.4 19.0 %collective-permute-start.21 = (bf16[1024,512]{1,0:T(8,128)(2,1)S(1)}, bf16[1024,512]{1,0:T(8,128)(2,1)S(1)}, u32[]{:S(2)}, u32[]{:S(2)}) collective-permute-start(bf16[1024,512]{1,0:T(8,128)(2,1)S(1)} %slice_select_fusion), channel_id=1, source_target_pairs={{0,96},{1,97},{2,98},{3,99},{4,100},{5,101},{6,102},{7,103},{8,104... | collective-permute-start | bytes 3145736 | tf_op jit(solution)/shard_map/ppermute | solution.py:17
  104.1 18.3 %collective-permute-start.19 = (bf16[1024,512]{1,0:T(8,128)(2,1)S(1)}, bf16[1024,512]{1,0:T(8,128)(2,1)S(1)}, u32[]{:S(2)}, u32[]{:S(2)}) collective-permute-start(bf16[1024,512]{1,0:T(8,128)(2,1)S(1)} %slice_select_fusion), channel_id=1, source_target_pairs={{0,64},{1,65},{2,66},{3,67},{4,68},{5,69},{6,70},{7,71},{8,72},{9,... | collective-permute-start | bytes 3145736 | tf_op jit(solution)/shard_map/ppermute | solution.py:17
  104.8 24.7 %collective-permute-start.20 = (bf16[1024,512]{1,0:T(8,128)(2,1)S(1)}, bf16[1024,512]{1,0:T(8,128)(2,1)}, u32[]{:S(2)}, u32[]{:S(2)}) collective-permute-start(bf16[1024,512]{1,0:T(8,128)(2,1)S(1)} %slice_select_fusion), channel_id=1, source_target_pairs={{0,32},{1,33},{2,34},{3,35},{4,36},{5,37},{6,38},{7,39},{8,40},{9,... | collective-permute-start | bytes 3145736 | tf_op jit(solution)/shard_map/ppermute | solution.py:17
  106.4 6.3 %collective-permute-start.5 = (f32[128,128]{1,0:T(8,128)S(1)}, f32[128,128]{1,0:T(8,128)S(1)}, u32[]{:S(2)}, u32[]{:S(2)}) collective-permute-start(f32[128,128]{1,0:T(8,128)S(1)} %pad_maximum_fusion.3), channel_id=1, source_target_pairs={{0,2},{1,3},{2,0},{3,1},{4,6},{5,7},{6,4},{7,5},{8,10},{9,11},{10,... | collective-permute-start | bytes 196616 | tf_op jit(solution)/shard_map/ppermute | solution.py:17
  113.3 6.4 %collective-permute-start.6 = (f32[256,128]{1,0:T(8,128)}, f32[256,128]{1,0:T(8,128)S(1)}, u32[]{:S(2)}, u32[]{:S(2)}) collective-permute-start(f32[256,128]{1,0:T(8,128)} %pad_maximum_fusion.2), channel_id=1, source_target_pairs={{0,4},{1,5},{2,6},{3,7},{4,0},{5,1},{6,2},{7,3},{8,12},{9,13},{10,... | collective-permute-start | bytes 393224 | tf_op jit(solution)/shard_map/ppermute | solution.py:17
  119.8 12.5 %collective-permute-start.7 = (f32[512,128]{1,0:T(8,128)S(1)}, f32[512,128]{1,0:T(8,128)S(1)}, u32[]{:S(2)}, u32[]{:S(2)}) collective-permute-start(f32[512,128]{1,0:T(8,128)S(1)} %pad_maximum_fusion.1), channel_id=1, source_target_pairs={{0,8},{1,9},{2,10},{3,11},{4,12},{5,13},{6,14},{7,15},{16,24},{17,... | collective-permute-start | bytes 786440 | tf_op jit(solution)/shard_map/ppermute | solution.py:17
  131.0 14.3 %collective-permute-start.22 = (bf16[1024,512]{1,0:T(8,128)(2,1)S(1)}, bf16[1024,512]{1,0:T(8,128)(2,1)S(1)}, u32[]{:S(2)}, u32[]{:S(2)}) collective-permute-start(bf16[1024,512]{1,0:T(8,128)(2,1)S(1)} %add_select_fusion), channel_id=1, source_target_pairs={{0,16},{32,48},{64,80},{96,112},{1,17},{33,49},{65,81},{97,113},{2... | collective-permute-start | bytes 3145736 | tf_op jit(solution)/shard_map/ppermute | solution.py:17
  132.4 2.7 %collective-permute-start.10 = (f32[512,128]{1,0:T(8,128)S(1)}, f32[512,128]{1,0:T(8,128)S(1)}, u32[]{:S(2)}, u32[]{:S(2)}) collective-permute-start(f32[512,128]{1,0:T(8,128)S(1)} %broadcast_select_fusion.2), channel_id=1, source_target_pairs={{0,96},{1,97},{2,98},{3,99},{4,100},{5,101},{6,102},{7,103},{8,104... | collective-permute-start | bytes 786440 | tf_op jit(solution)/shard_map/ppermute | solution.py:17
  133.1 2.0 %collective-permute-start.8 = (f32[512,128]{1,0:T(8,128)S(1)}, f32[512,128]{1,0:T(8,128)S(1)}, u32[]{:S(2)}, u32[]{:S(2)}) collective-permute-start(f32[512,128]{1,0:T(8,128)S(1)} %broadcast_select_fusion.2), channel_id=1, source_target_pairs={{0,64},{1,65},{2,66},{3,67},{4,68},{5,69},{6,70},{7,71},{8,72},{9,... | collective-permute-start | bytes 786440 | tf_op jit(solution)/shard_map/ppermute | solution.py:17
  133.8 8.3 %collective-permute-start.9 = (f32[512,128]{1,0:T(8,128)S(1)}, f32[512,128]{1,0:T(8,128)S(1)}, u32[]{:S(2)}, u32[]{:S(2)}) collective-permute-start(f32[512,128]{1,0:T(8,128)S(1)} %broadcast_select_fusion.2), channel_id=1, source_target_pairs={{0,32},{1,33},{2,34},{3,35},{4,36},{5,37},{6,38},{7,39},{8,40},{9,... | collective-permute-start | bytes 786440 | tf_op jit(solution)/shard_map/ppermute | solution.py:17
  142.1 2.4 %collective-permute-start.11 = (f32[512,128]{1,0:T(8,128)S(1)}, f32[512,128]{1,0:T(8,128)S(1)}, u32[]{:S(2)}, u32[]{:S(2)}) collective-permute-start(f32[512,128]{1,0:T(8,128)S(1)} %add_select_fusion.2), channel_id=1, source_target_pairs={{0,16},{32,48},{64,80},{96,112},{1,17},{33,49},{65,81},{97,113},{2... | collective-permute-start | bytes 786440 | tf_op jit(solution)/shard_map/ppermute | solution.py:17
  149.2 22.8 %collective-permute-start.23 = (f32[64,128]{1,0:T(8,128)}, f32[64,128]{1,0:T(8,128)S(1)}, u32[]{:S(2)}, u32[]{:S(2)}) collective-permute-start(f32[64,128]{1,0:T(8,128)} %shard_map.87), channel_id=1, source_target_pairs={{0,16},{16,32},{32,48},{48,64},{64,80},{80,96},{96,112},{1,17},{17... | collective-permute-start | bytes 98312 | tf_op jit(solution)/shard_map/ppermute | solution.py:17
  151.4 20.6 %collective-permute-start.24 = (f32[64,128]{1,0:T(8,128)}, f32[64,128]{1,0:T(8,128)S(1)}, u32[]{:S(2)}, u32[]{:S(2)}) collective-permute-start(f32[64,128]{1,0:T(8,128)} %shard_map.87), channel_id=1, source_target_pairs={{16,0},{32,16},{48,32},{64,48},{80,64},{96,80},{112,96},{17,1},{33... | collective-permute-start | bytes 98312 | tf_op jit(solution)/shard_map/ppermute | solution.py:17
  154.8 17.3 %collective-permute-start.25 = (f32[64,128]{1,0:T(8,128)}, f32[64,128]{1,0:T(8,128)S(1)}, u32[]{:S(2)}, u32[]{:S(2)}) collective-permute-start(f32[64,128]{1,0:T(8,128)} %shard_map.87), channel_id=1, source_target_pairs={{0,1},{1,2},{2,3},{3,4},{4,5},{5,6},{6,7},{7,8},{8,9},{9,10},{10,1... | collective-permute-start | bytes 98312 | tf_op jit(solution)/shard_map/ppermute | solution.py:17
  157.7 14.3 %collective-permute-start.26 = (f32[64,128]{1,0:T(8,128)}, f32[64,128]{1,0:T(8,128)S(1)}, u32[]{:S(2)}, u32[]{:S(2)}) collective-permute-start(f32[64,128]{1,0:T(8,128)} %shard_map.87), channel_id=1, source_target_pairs={{1,0},{2,1},{3,2},{4,3},{5,4},{6,5},{7,6},{8,7},{9,8},{10,9},{11,1... | collective-permute-start | bytes 98312 | tf_op jit(solution)/shard_map/ppermute | solution.py:17
  162.8 9.3 %copy-start.9 = (s32[4,128]{1,0:T(4,128)S(1)}, s32[4,128]{1,0:T(4,128)}, u32[]{:S(2)}) copy-start(s32[4,128]{1,0:T(4,128)} %param.11) | copy-start | bytes 6148
  162.8 9.7 %copy-start.7 = (f32[64,128]{1,0:T(8,128)S(1)}, f32[64,128]{1,0:T(8,128)}, u32[]{:S(2)}) copy-start(f32[64,128]{1,0:T(8,128)} %shard_map.87) | copy-start | bytes 98308
  (8 other events, 44.4 us)
Sparse Core Ops, SparseCore 0:
  102.5 53.2 all-gather.2

commit v4 on v3

--- a/solution.py
+++ b/solution.py
@@ -25,13 +25,16 @@
     return jnp.where(row == 0, value, got[0] + got[1] + got[2])
 
 
+def exchange(value, col, bit):
+    other = send(value, "col", [(at, at ^ bit) for at in range(16)])
+    after = (col & bit) == 0
+    return jnp.concatenate(
+        [jnp.where(after, value, other), jnp.where(after, other, value)], axis=0
+    )
+
+
 def gather_first_half(value, col):
-    for bit in (1, 2, 4):
-        other = send(value, "col", [(at, at ^ bit) for at in range(16)])
-        after = (col & bit) == 0
-        value = jnp.concatenate(
-            [jnp.where(after, value, other), jnp.where(after, other, value)], axis=0
-        )
+    value = exchange(exchange(value, col, 2), col, 4)
     return jnp.where(col < 8, value, send(value, "col", [(at, at + 8) for at in range(8)]))
 
 
@@ -43,34 +46,39 @@
 
 
 def lift_kernel(table_ref, *refs):
-    tiles, (mixed_ref, inverses_ref), outs = refs[:4], refs[4:6], refs[6:]
+    lows, tiles, (mixed_ref, inverses_ref), outs = refs[:4], refs[4:8], refs[8:10], refs[10:14]
+    cross_ref = refs[14]
     panel = inverses_ref.shape[1]
+
+    @pl.when(pl.program_id(0) == 0)
+    def _():
+        cross_ref[...] = multiply(mixed_ref[:panel], inverses_ref[0]).astype(BF16)
+
+    low0 = jnp.concatenate([low_ref[...] for low_ref in lows], axis=0)
     rows = jnp.concatenate([tile_ref[...] for tile_ref in tiles], axis=0)
-    first, second = inverses_ref[0], inverses_ref[1]
-    cross = multiply(mixed_ref[:panel], first).astype(BF16)
-    low0 = multiply(rows[:, :panel], first).astype(BF16)
-    low1 = rows[:, panel:].astype(F32) - multiply(low0, mixed_ref[panel:])
-    low1 = multiply(low1.astype(BF16), second).astype(BF16)
-    low0 = (low0.astype(F32) - multiply(low1, cross)).astype(BF16)
-    done = jnp.concatenate([low0, low1], axis=1)
+    low1 = rows.astype(F32) - multiply(low0, mixed_ref[panel:])
+    low1 = multiply(low1.astype(BF16), inverses_ref[1]).astype(BF16)
+    low0 = (low0.astype(F32) - multiply(low1, cross_ref[...])).astype(BF16)
     for which, out_ref in enumerate(outs):
 
         @pl.when(pl.program_id(0) == which)
         def _(out_ref=out_ref):
-            out_ref[...] = done
-
-
-def lift(panels, mixed, inverses, tile):
-    depth = inverses.shape[0] * inverses.shape[1]
+            out_ref[:, :panel] = low0
+            out_ref[:, panel:] = low1
+
+
+def lift(low0, panels, mixed, inverses, tile):
+    panel = inverses.shape[1]
     table = jnp.array([at for members in REGIONS for at in members], dtype=jnp.int32)
-    bundle = jax.ShapeDtypeStruct((4 * tile, depth), BF16)
+    bundle = jax.ShapeDtypeStruct((4 * tile, 2 * panel), BF16)
     return pl.pallas_call(
         lift_kernel,
         grid_spec=pltpu.PrefetchScalarGridSpec(
             num_scalar_prefetch=1,
             grid=(4,),
             in_specs=[
-                pl.BlockSpec((tile, depth), lambda i, table, j=j: (table[4 * i + j], 0))
+                pl.BlockSpec((tile, panel), lambda i, table, j=j, at=at: (table[4 * i + j], at))
+                for at in range(2)
                 for j in range(4)
             ]
             + [
@@ -78,10 +86,11 @@
                 pl.BlockSpec(inverses.shape, lambda i, table: (0, 0, 0)),
             ],
             out_specs=[pl.BlockSpec(bundle.shape, lambda i, table: (0, 0)) for _ in REGIONS],
+            scratch_shapes=[pltpu.VMEM((panel, panel), BF16)],
         ),
         out_shape=[bundle] * 4,
-        compiler_params=pltpu.CompilerParams(vmem_limit_bytes=40 << 20),
-    )(table, *([panels] * 4), mixed, inverses)
+        compiler_params=pltpu.CompilerParams(vmem_limit_bytes=56 << 20),
+    )(table, *([low0] * 4), *([panels] * 4), mixed, inverses)
 
 
 def pass_on(bundles, col, tile):
@@ -127,7 +136,7 @@
 def update(base, low, mixed, plain):
     rows, width = base.shape
     tiles, tile, depth = low.shape
-    group = 4
+    group = 8
     step = group * tile
     return pl.pallas_call(
         update_kernel,
@@ -171,13 +180,16 @@
         raw.reshape(sources, cols, tile), "col", split_axis=1, concat_axis=0, tiled=True
     )
     raw_tile = jnp.sum(swapped.reshape(cols, sources, tile).astype(F32), axis=0)
-    mixed_lines, raw_tile = lax.optimization_barrier((mixed_lines, raw_tile))
+    low0 = multiply(matrix[:, :panel], inverses[0]).astype(BF16)
+    mixed_lines, raw_tile, low0 = lax.optimization_barrier((mixed_lines, raw_tile, low0))
     mixed = on_even(mixed, mixed_lines, row)
     mixed = jnp.where(even, mixed, to_odd(mixed))
 
-    bundles = lift(matrix, mixed, inverses, tile)
-    bundles, raw_tile = lax.optimization_barrier((bundles, raw_tile))
-    parts = gather_first_half(raw_tile, col)
+    pair = exchange(raw_tile, col, 1)
+    mixed, pair = lax.optimization_barrier((mixed, pair))
+    bundles = lift(low0, matrix, mixed, inverses, tile)
+    bundles, pair = lax.optimization_barrier((bundles, pair))
+    parts = gather_first_half(pair, col)
     piece = pass_on(bundles, col, tile)
     piece, plain = lax.optimization_barrier((piece, plain))
     low = lax.all_gather(piece, "col")

time: 181 us -> 178 us (0.983)
  waiting for transfers between devices: 73.5 us -> 66.3 us
  matrix products: 4.14 us -> 8.39 us
  local copies, waits for them, and re-layouts: 3.6 us -> 1.4 us
  other arithmetic: 10.8 us -> 12.8 us
    all_to_all x1, waiting for transfers between devices: 7.07 us -> 2.9 us  [shards(): lax.all_to_all(raw.reshape(sources, cols, tile), 'col', split_axis=1, con...]
    dot_general x0 -> x1, matrix products: none -> 4.16 us  [multiply(): return jnp.dot(left, right, preferred_element_type=F32)]
    ppermute x27, waiting for transfers between devices: 66.4 us -> 63.3 us  [send(): return lax.ppermute(value, axis, pairs)]
    unnamed x22 -> x16, local copies, waits for them, and re-layouts: 2.23 us -> 0.04 us
  transfers between devices with their start and end apart: 29 -> 29, of which waited for: 12 -> 11; matrix products, arithmetic and copies ran while one was open for 5% -> 7% of each run, Pallas kernels for 7% -> 7%
where the time goes in v4:
time: 178 us; the launch traced here: 177 us
  waiting for transfers between devices  66.3 us (37%)
  starting transfers between devices  51.8 us (29%)
  Pallas kernels  21.8 us (12%)
  between operations  14.5 us (8%)
  other arithmetic  12.8 us (7%)
  matrix products  8.39 us (5%)
    ppermute x27, waiting for transfers between devices, send(): return lax.ppermute(value, axis, pairs)  63.3 us
    ppermute x27, starting transfers between devices, send(): return lax.ppermute(value, axis, pairs)  43.7 us
    pallas_call x1, Pallas kernels, lift(): pl.pallas_call(lift_kernel, grid_spec=pltpu.PrefetchScalarGridSpec(num_sc...  10.1 us
    pallas_call x1, Pallas kernels, update(): pl.pallas_call(update_kernel, grid=(rows // step,), in_specs=[pl.BlockSpe...  8.99 us
    all_to_all x1, starting transfers between devices, shards(): lax.all_to_all(raw.reshape(sources, cols, tile), 'col', split_axis=1, con...  8.07 us
    dot_general x1, matrix products, multiply(): return jnp.dot(left, right, preferred_element_type=F32)  4.16 us
    select_n x3, other arithmetic, on_even(): return jnp.where(row == 0, value, got[0] + got[1] + got[2])  3.89 us
    dot_general x1, matrix products, shards(): lax.dot_general(stacked, matrix, (((1,), (1,)), ((), ())), preferred_elem...  3.79 us
  transfers between devices with their start and end apart: 29, of which 11 were waited for; matrix products, arithmetic and copies ran while one was open for 7% of the time, Pallas kernels for 7%

profile of v4, /device:TPU:34, one launch (start us, length us, event | category | flops | bytes accessed | tf_op | source)
XLA Modules:
  0.0 177.0 jit_solution(3885541153779414717)
XLA Ops:
  8.6 1.6 collective-permute-start
  11.5 1.6 collective-permute-start.2
  13.3 3.8 %fusion.9 = f32[128,2048]{1,0:T(8,128)S(1)} fusion(bf16[2048,1024]{1,0:T(8,128)(2,1)} %base_ref.1, bf16[64,1024]{1,0:T(8,128)(2,1)S(1)} %compare_convert_fusion, bf16[64,1024]{1,0:T(8,128)(2,1)S(1)} %copy-done.3), kind=kOutput, calls=%fused_computation.22 | convolution fusion | flops 537395200 | bytes 5505024 | tf_op jit(solution)/shard_map/dot_general | solution.py:175
  17.8 8.1 %all-to-all-start = ((bf16[64,16,128]{2,0,1:T(8,128)(2,1)}), bf16[64,16,128]{2,0,1:T(8,128)(2,1)S(1)}, u32[]{:S(2)}, u32[]{:S(2)}) async-start(bf16[64,16,128]{2,0,1:T(8,128)(2,1)} %copy_bitcast_fusion), calls=%async_computation | async-start | bytes 524288 | tf_op jit(solution)/shard_map/all_to_all | solution.py:179
  26.0 4.2 %convolution_convert_fusion.refs_0_.refs_1_.refs_2_.refs_3_ = bf16[2048,512]{1,0:T(8,128)(2,1)} fusion(bf16[2048,1024]{1,0:T(8,128)(2,1)} %base_ref.1, bf16[2,512,512]{2,1,0:T(8,128)(2,1)S(1)} %copy-done.1), kind=kOutput, calls=%fused_computation | convolution fusion | flops 1074790400 | bytes 4718592 | tf_op jit(solution)/shard_map/dot_general | solution.py:13
  30.1 2.9 %all-to-all-done = bf16[64,16,128]{2,0,1:T(8,128)(2,1)S(1)} async-done(((bf16[64,16,128]{2,0,1:T(8,128)(2,1)}), bf16[64,16,128]{2,0,1:T(8,128)(2,1)S(1)}, u32[]{:S(2)}, u32[]{:S(2)}) %all-to-all-start) | async-done | bytes 262176 | tf_op jit(solution)/shard_map/all_to_all | solution.py:179
  33.1 5.0 %collective-permute-done.1 = bf16[1024,512]{1,0:T(8,128)(2,1)} collective-permute-done((bf16[1024,512]{1,0:T(8,128)(2,1)S(1)}, bf16[1024,512]{1,0:T(8,128)(2,1)}, u32[]{:S(2)}, u32[]{:S(2)}) %collective-permute-start.1) | collective-permute-done | bytes 1048608 | tf_op jit(solution)/shard_map/ppermute | solution.py:17
  38.1 2.4 %add_select_fusion.1 = bf16[1024,512]{1,0:T(8,128)(2,1)S(1)} fusion(bf16[1024,512]{1,0:T(8,128)(2,1)} %collective-permute-done.2, bf16[1024,512]{1,0:T(8,128)(2,1)} %collective-permute-done, bf16[1024,512]{1,0:T(8,128)(2,1)} %collective-permute-done.1, pred[]{:T(512)S(6)} %eq.46, bf16[512,512]{1,0:T(8,128)(2,1)S(1)} %get-tuple-element.53, ...), kind=kLoop, calls=%fused_computation.8 | loop fusion | flops 5767168 | bytes 5242881 | tf_op jit(solution)/shard_map/jit(_where)/select_n | solution.py:25
  40.6 1.4 collective-permute-start.3
  41.9 1.7 collective-permute-start.4
  43.6 2.3 %collective-permute-done.4 = f32[64,128]{1,0:T(8,128)S(1)} collective-permute-done((f32[64,128]{1,0:T(8,128)S(1)}, f32[64,128]{1,0:T(8,128)S(1)}, u32[]{:S(2)}, u32[]{:S(2)}) %collective-permute-start.4) | collective-permute-done | bytes 32800 | tf_op jit(solution)/shard_map/ppermute | solution.py:17
  47.1 10.1 %shard_map.86 = (bf16[512,1024]{1,0:T(8,128)(2,1)}, bf16[512,1024]{1,0:T(8,128)(2,1)}, bf16[512,1024]{1,0:T(8,128)(2,1)}, bf16[512,1024]{1,0:T(8,128)(2,1)}) custom-call(s32[16]{0:T(128)} %constant.36.clone.table_ref, bf16[2048,512]{1,0:T(8,128)(2,1)} %convolution_convert_fusion.refs_0_.refs_1_.refs_2_.refs_3_, ...), custom_call_target="tpu_custom_call" | custom-call | tf_op jit(solution)/shard_map/pallas_call | solution.py:74
  59.9 1.7 collective-permute-start.13
  61.6 24.7 %collective-permute-done.14 = bf16[512,1024]{1,0:T(8,128)(2,1)S(1)} collective-permute-done((bf16[512,1024]{1,0:T(8,128)(2,1)}, bf16[512,1024]{1,0:T(8,128)(2,1)S(1)}, u32[]{:S(2)}, u32[]{:S(2)}) %collective-permute-start.14) | collective-permute-done | bytes 1048608 | tf_op jit(solution)/shard_map/ppermute | solution.py:17
  86.3 1.6 add_add_fusion
  92.1 3.6 %collective-permute-done.18 = bf16[128,1024]{1,0:T(8,128)(2,1)S(1)} collective-permute-done((bf16[128,1024]{1,0:T(8,128)(2,1)S(1)}, bf16[128,1024]{1,0:T(8,128)(2,1)S(1)}, u32[]{:S(2)}, u32[]{:S(2)}) %collective-permute-start.18) | collective-permute-done | bytes 262176 | tf_op jit(solution)/shard_map/ppermute | solution.py:17
  95.7 2.8 %collective-permute-done.17 = bf16[128,1024]{1,0:T(8,128)(2,1)S(1)} collective-permute-done((bf16[128,1024]{1,0:T(8,128)(2,1)S(1)}, bf16[128,1024]{1,0:T(8,128)(2,1)S(1)}, u32[]{:S(2)}, u32[]{:S(2)}) %collective-permute-start.17) | collective-permute-done | bytes 262176 | tf_op jit(solution)/shard_map/ppermute | solution.py:17
  98.5 1.7 fusion.8.piece_ref
  103.0 4.1 %collective-permute-start.5 = (f32[128,128]{1,0:T(8,128)S(1)}, f32[128,128]{1,0:T(8,128)S(1)}, u32[]{:S(2)}, u32[]{:S(2)}) collective-permute-start(f32[128,128]{1,0:T(8,128)S(1)} %pad_maximum_fusion.3), channel_id=1, source_target_pairs={{0,2},{1,3},{2,0},{3,1},{4,6},{5,7},{6,4},{7,5},{8,10},{9,11},{10,... | collective-permute-start | bytes 196616 | tf_op jit(solution)/shard_map/ppermute | solution.py:17
  107.1 2.2 %collective-permute-done.5 = f32[128,128]{1,0:T(8,128)S(1)} collective-permute-done((f32[128,128]{1,0:T(8,128)S(1)}, f32[128,128]{1,0:T(8,128)S(1)}, u32[]{:S(2)}, u32[]{:S(2)}) %collective-permute-start.5) | collective-permute-done | bytes 65568 | tf_op jit(solution)/shard_map/ppermute | solution.py:17
  110.0 6.4 %collective-permute-done.6 = f32[256,128]{1,0:T(8,128)S(1)} collective-permute-done((f32[256,128]{1,0:T(8,128)}, f32[256,128]{1,0:T(8,128)S(1)}, u32[]{:S(2)}, u32[]{:S(2)}) %collective-permute-start.6) | collective-permute-done | bytes 131104 | tf_op jit(solution)/shard_map/ppermute | solution.py:17
  116.4 2.2 %collective-permute-start.7 = (f32[512,128]{1,0:T(8,128)S(1)}, f32[512,128]{1,0:T(8,128)S(1)}, u32[]{:S(2)}, u32[]{:S(2)}) collective-permute-start(f32[512,128]{1,0:T(8,128)S(1)} %pad_maximum_fusion.1), channel_id=1, source_target_pairs={{0,8},{1,9},{2,10},{3,11},{4,12},{5,13},{6,14},{7,15},{16,24},{17,... | collective-permute-start | bytes 786440 | tf_op jit(solution)/shard_map/ppermute | solution.py:17
  118.6 8.1 %collective-permute-done.20 = bf16[1024,512]{1,0:T(8,128)(2,1)} collective-permute-done((bf16[1024,512]{1,0:T(8,128)(2,1)S(1)}, bf16[1024,512]{1,0:T(8,128)(2,1)}, u32[]{:S(2)}, u32[]{:S(2)}) %collective-permute-start.20) | collective-permute-done | bytes 1048608 | tf_op jit(solution)/shard_map/ppermute | solution.py:17
  126.8 1.4 add_select_fusion
  128.2 1.4 collective-permute-start.22
  132.3 6.9 %collective-permute-done.9 = f32[512,128]{1,0:T(8,128)S(1)} collective-permute-done((f32[512,128]{1,0:T(8,128)S(1)}, f32[512,128]{1,0:T(8,128)S(1)}, u32[]{:S(2)}, u32[]{:S(2)}) %collective-permute-start.9) | collective-permute-done | bytes 262176 | tf_op jit(solution)/shard_map/ppermute | solution.py:17
  143.6 2.8 %shard_map.87 = f32[64,128]{1,0:T(8,128)} custom-call(f32[64,128]{1,0:T(8,128)} %copy-done.2, f32[512,128]{1,0:T(8,128)} %broadcast_select_fusion.3.parts_ref, bf16[128,1024]{1,0:T(8,128)(2,1)} %fusion.8.piece_ref), custom_call_target="tpu_custom_call" | custom-call | tf_op jit(solution)/shard_map/pallas_call | solution.py:203
  146.4 2.3 %collective-permute-start.23 = (f32[64,128]{1,0:T(8,128)}, f32[64,128]{1,0:T(8,128)S(1)}, u32[]{:S(2)}, u32[]{:S(2)}) collective-permute-start(f32[64,128]{1,0:T(8,128)} %shard_map.87), channel_id=1, source_target_pairs={{0,16},{16,32},{32,48},{48,64},{64,80},{80,96},{96,112},{1,17},{17... | collective-permute-start | bytes 98312 | tf_op jit(solution)/shard_map/ppermute | solution.py:17
  148.7 3.3 %collective-permute-start.24 = (f32[64,128]{1,0:T(8,128)}, f32[64,128]{1,0:T(8,128)S(1)}, u32[]{:S(2)}, u32[]{:S(2)}) collective-permute-start(f32[64,128]{1,0:T(8,128)} %shard_map.87), channel_id=1, source_target_pairs={{16,0},{32,16},{48,32},{64,48},{80,64},{96,80},{112,96},{17,1},{33... | collective-permute-start | bytes 98312 | tf_op jit(solution)/shard_map/ppermute | solution.py:17
  152.0 3.0 %collective-permute-start.25 = (f32[64,128]{1,0:T(8,128)}, f32[64,128]{1,0:T(8,128)S(1)}, u32[]{:S(2)}, u32[]{:S(2)}) collective-permute-start(f32[64,128]{1,0:T(8,128)} %shard_map.87), channel_id=1, source_target_pairs={{0,1},{1,2},{2,3},{3,4},{4,5},{5,6},{6,7},{7,8},{8,9},{9,10},{10,1... | collective-permute-start | bytes 98312 | tf_op jit(solution)/shard_map/ppermute | solution.py:17
  155.0 4.9 %collective-permute-start.26 = (f32[64,128]{1,0:T(8,128)}, f32[64,128]{1,0:T(8,128)S(1)}, u32[]{:S(2)}, u32[]{:S(2)}) collective-permute-start(f32[64,128]{1,0:T(8,128)} %shard_map.87), channel_id=1, source_target_pairs={{1,0},{2,1},{3,2},{4,3},{5,4},{6,5},{7,6},{8,7},{9,8},{10,9},{11,1... | collective-permute-start | bytes 98312 | tf_op jit(solution)/shard_map/ppermute | solution.py:17
  160.0 9.0 %shard_map.88 = bf16[2048,1024]{1,0:T(8,128)(2,1)} custom-call(bf16[2048,1024]{1,0:T(8,128)(2,1)} %base_ref.1, bf16[16,128,1024]{2,1,0:T(8,128)(2,1)} %bitcast.14, bf16[1024,512]{1,0:T(8,128)(2,1)} %broadcast_select_fusion.1.refs_8_.mixed_ref, bf16[1024,512]{1,0:T(8,128)(2,1)} %broadcast_select_fusion.plain_ref), custom_call_target="tpu_custom_call" | custom-call | tf_op jit(solution)/shard_map/pallas_call | solution.py:141
  (74 shorter events, 23.3 us)
Async XLA Ops:
  8.6 24.5 %collective-permute-start = (bf16[1024,512]{1,0:T(8,128)(2,1)S(1)}, bf16[1024,512]{1,0:T(8,128)(2,1)}, u32[]{:S(2)}, u32[]{:S(2)}) collective-permute-start(bf16[1024,512]{1,0:T(8,128)(2,1)S(1)} %pad_maximum_fusion), channel_id=1, source_target_pairs={{0,64},{1,65},{2,66},{3,67},{4,68},{5,69},{6,70},{7,71},{8,72},{9,... | collective-permute-start | bytes 3145736 | tf_op jit(solution)/shard_map/ppermute | solution.py:17
  10.2 27.9 %collective-permute-start.1 = (bf16[1024,512]{1,0:T(8,128)(2,1)S(1)}, bf16[1024,512]{1,0:T(8,128)(2,1)}, u32[]{:S(2)}, u32[]{:S(2)}) collective-permute-start(bf16[1024,512]{1,0:T(8,128)(2,1)S(1)} %pad_maximum_fusion), channel_id=1, source_target_pairs={{0,32},{1,33},{2,34},{3,35},{4,36},{5,37},{6,38},{7,39},{8,40},{9,... | collective-permute-start | bytes 3145736 | tf_op jit(solution)/shard_map/ppermute | solution.py:17
  11.5 26.6 %collective-permute-start.2 = (bf16[1024,512]{1,0:T(8,128)(2,1)S(1)}, bf16[1024,512]{1,0:T(8,128)(2,1)}, u32[]{:S(2)}, u32[]{:S(2)}) collective-permute-start(bf16[1024,512]{1,0:T(8,128)(2,1)S(1)} %pad_maximum_fusion), channel_id=1, source_target_pairs={{0,96},{1,97},{2,98},{3,99},{4,100},{5,101},{6,102},{7,103},{8,104... | collective-permute-start | bytes 3145736 | tf_op jit(solution)/shard_map/ppermute | solution.py:17
  13.3 12.7 %copy-start.1 = (bf16[2,512,512]{2,1,0:T(8,128)(2,1)S(1)}, bf16[2,512,512]{2,1,0:T(8,128)(2,1)}, u32[]{:S(2)}) copy-start(bf16[2,512,512]{2,1,0:T(8,128)(2,1)} %refs_9_.1) | copy-start | bytes 3145732
  17.8 15.2 %all-to-all-start = ((bf16[64,16,128]{2,0,1:T(8,128)(2,1)}), bf16[64,16,128]{2,0,1:T(8,128)(2,1)S(1)}, u32[]{:S(2)}, u32[]{:S(2)}) async-start(bf16[64,16,128]{2,0,1:T(8,128)(2,1)} %copy_bitcast_fusion), calls=%async_computation | async-start | bytes 524288 | tf_op jit(solution)/shard_map/all_to_all | solution.py:179
  25.9 134.0 %all-gather.3.cloned.1.call-start = ((), (), s32[]{:S(2)}) async-start(), calls=%async_computation.1 | async-start | bytes 4456448 | tf_op jit(solution)/shard_map/all_gather | solution.py:195
  33.1 12.9 %copy-start.2 = (f32[64,128]{1,0:T(8,128)}, f32[64,128]{1,0:T(8,128)S(1)}, u32[]{:S(2)}) copy-start(f32[64,128]{1,0:T(8,128)S(1)} %convert_reduce_fusion.raw_ref) | copy-start | bytes 98308
  40.6 5.4 %collective-permute-start.3 = (bf16[1024,512]{1,0:T(8,128)(2,1)S(1)}, bf16[1024,512]{1,0:T(8,128)(2,1)S(1)}, u32[]{:S(2)}, u32[]{:S(2)}) collective-permute-start(bf16[1024,512]{1,0:T(8,128)(2,1)S(1)} %add_select_fusion.1), channel_id=1, source_target_pairs={{0,16},{32,48},{64,80},{96,112},{1,17},{33,49},{65,81},{97,113},{2... | collective-permute-start | bytes 3145736 | tf_op jit(solution)/shard_map/ppermute | solution.py:17
  41.9 4.0 %collective-permute-start.4 = (f32[64,128]{1,0:T(8,128)S(1)}, f32[64,128]{1,0:T(8,128)S(1)}, u32[]{:S(2)}, u32[]{:S(2)}) collective-permute-start(f32[64,128]{1,0:T(8,128)S(1)} %convert_reduce_fusion.raw_ref), channel_id=1, source_target_pairs={{0,1},{1,0},{2,3},{3,2},{4,5},{5,4},{6,7},{7,6},{8,9},{9,8},{10,11... | collective-permute-start | bytes 98312 | tf_op jit(solution)/shard_map/ppermute | solution.py:17
  57.1 4.4 %collective-permute-start.15 = (bf16[512,1024]{1,0:T(8,128)(2,1)}, bf16[512,1024]{1,0:T(8,128)(2,1)S(1)}, u32[]{:S(2)}, u32[]{:S(2)}) collective-permute-start(bf16[512,1024]{1,0:T(8,128)(2,1)} %get-tuple-element.42), channel_id=1, source_target_pairs={{0,12},{16,28},{32,44},{48,60},{64,76},{80,92},{96,108},{112,124}} | collective-permute-start | bytes 3145736 | tf_op jit(solution)/shard_map/ppermute | solution.py:17
  57.9 28.5 %collective-permute-start.14 = (bf16[512,1024]{1,0:T(8,128)(2,1)}, bf16[512,1024]{1,0:T(8,128)(2,1)S(1)}, u32[]{:S(2)}, u32[]{:S(2)}) collective-permute-start(bf16[512,1024]{1,0:T(8,128)(2,1)} %get-tuple-element.41), channel_id=1, source_target_pairs={{0,4},{16,20},{32,36},{48,52},{64,68},{80,84},{96,100},{112,116}} | collective-permute-start | bytes 3145736 | tf_op jit(solution)/shard_map/ppermute | solution.py:17
  59.2 27.2 %collective-permute-start.12 = (bf16[512,1024]{1,0:T(8,128)(2,1)}, bf16[512,1024]{1,0:T(8,128)(2,1)S(1)}, u32[]{:S(2)}, u32[]{:S(2)}) collective-permute-start(bf16[512,1024]{1,0:T(8,128)(2,1)} %get-tuple-element.40), channel_id=1, source_target_pairs={{0,1},{16,17},{32,33},{48,49},{64,65},{80,81},{96,97},{112,113}} | collective-permute-start | bytes 3145736 | tf_op jit(solution)/shard_map/ppermute | solution.py:17
  59.9 26.4 %collective-permute-start.13 = (bf16[512,1024]{1,0:T(8,128)(2,1)}, bf16[512,1024]{1,0:T(8,128)(2,1)}, u32[]{:S(2)}, u32[]{:S(2)}) collective-permute-start(bf16[512,1024]{1,0:T(8,128)(2,1)} %get-tuple-element.39), channel_id=1, source_target_pairs={{0,3},{16,19},{32,35},{48,51},{64,67},{80,83},{96,99},{112,115}} | collective-permute-start | bytes 3145736 | tf_op jit(solution)/shard_map/ppermute | solution.py:17
  88.0 7.7 %collective-permute-start.18 = (bf16[128,1024]{1,0:T(8,128)(2,1)S(1)}, bf16[128,1024]{1,0:T(8,128)(2,1)S(1)}, u32[]{:S(2)}, u32[]{:S(2)}) collective-permute-start(bf16[128,1024]{1,0:T(8,128)(2,1)S(1)} %get-tuple-element.55), channel_id=1, source_target_pairs={{1,2},{4,9},{12,10},{17,18},{20,25},{28,26},{33,34},{36,41},{44,42... | collective-permute-start | bytes 786440 | tf_op jit(solution)/shard_map/ppermute | solution.py:17
  89.3 9.2 %collective-permute-start.17 = (bf16[128,1024]{1,0:T(8,128)(2,1)S(1)}, bf16[128,1024]{1,0:T(8,128)(2,1)S(1)}, u32[]{:S(2)}, u32[]{:S(2)}) collective-permute-start(bf16[128,1024]{1,0:T(8,128)(2,1)S(1)} %get-tuple-element.56), channel_id=1, source_target_pairs={{1,13},{3,15},{4,6},{12,11},{17,29},{19,31},{20,22},{28,27},{33,45... | collective-permute-start | bytes 786440 | tf_op jit(solution)/shard_map/ppermute | solution.py:17
  90.6 7.9 %collective-permute-start.16 = (bf16[128,1024]{1,0:T(8,128)(2,1)S(1)}, bf16[128,1024]{1,0:T(8,128)(2,1)S(1)}, u32[]{:S(2)}, u32[]{:S(2)}) collective-permute-start(bf16[128,1024]{1,0:T(8,128)(2,1)S(1)} %get-tuple-element.54), channel_id=1, source_target_pairs={{1,5},{3,7},{4,8},{12,14},{17,21},{19,23},{20,24},{28,30},{33,37},... | collective-permute-start | bytes 786440 | tf_op jit(solution)/shard_map/ppermute | solution.py:17
  100.3 18.3 %collective-permute-start.21 = (bf16[1024,512]{1,0:T(8,128)(2,1)S(1)}, bf16[1024,512]{1,0:T(8,128)(2,1)S(1)}, u32[]{:S(2)}, u32[]{:S(2)}) collective-permute-start(bf16[1024,512]{1,0:T(8,128)(2,1)S(1)} %slice_select_fusion), channel_id=1, source_target_pairs={{0,96},{1,97},{2,98},{3,99},{4,100},{5,101},{6,102},{7,103},{8,104... | collective-permute-start | bytes 3145736 | tf_op jit(solution)/shard_map/ppermute | solution.py:17
  101.0 17.6 %collective-permute-start.19 = (bf16[1024,512]{1,0:T(8,128)(2,1)S(1)}, bf16[1024,512]{1,0:T(8,128)(2,1)S(1)}, u32[]{:S(2)}, u32[]{:S(2)}) collective-permute-start(bf16[1024,512]{1,0:T(8,128)(2,1)S(1)} %slice_select_fusion), channel_id=1, source_target_pairs={{0,64},{1,65},{2,66},{3,67},{4,68},{5,69},{6,70},{7,71},{8,72},{9,... | collective-permute-start | bytes 3145736 | tf_op jit(solution)/shard_map/ppermute | solution.py:17
  101.7 25.0 %collective-permute-start.20 = (bf16[1024,512]{1,0:T(8,128)(2,1)S(1)}, bf16[1024,512]{1,0:T(8,128)(2,1)}, u32[]{:S(2)}, u32[]{:S(2)}) collective-permute-start(bf16[1024,512]{1,0:T(8,128)(2,1)S(1)} %slice_select_fusion), channel_id=1, source_target_pairs={{0,32},{1,33},{2,34},{3,35},{4,36},{5,37},{6,38},{7,39},{8,40},{9,... | collective-permute-start | bytes 3145736 | tf_op jit(solution)/shard_map/ppermute | solution.py:17
  103.0 6.3 %collective-permute-start.5 = (f32[128,128]{1,0:T(8,128)S(1)}, f32[128,128]{1,0:T(8,128)S(1)}, u32[]{:S(2)}, u32[]{:S(2)}) collective-permute-start(f32[128,128]{1,0:T(8,128)S(1)} %pad_maximum_fusion.3), channel_id=1, source_target_pairs={{0,2},{1,3},{2,0},{3,1},{4,6},{5,7},{6,4},{7,5},{8,10},{9,11},{10,... | collective-permute-start | bytes 196616 | tf_op jit(solution)/shard_map/ppermute | solution.py:17
  110.0 6.4 %collective-permute-start.6 = (f32[256,128]{1,0:T(8,128)}, f32[256,128]{1,0:T(8,128)S(1)}, u32[]{:S(2)}, u32[]{:S(2)}) collective-permute-start(f32[256,128]{1,0:T(8,128)} %pad_maximum_fusion.2), channel_id=1, source_target_pairs={{0,4},{1,5},{2,6},{3,7},{4,0},{5,1},{6,2},{7,3},{8,12},{9,13},{10,... | collective-permute-start | bytes 393224 | tf_op jit(solution)/shard_map/ppermute | solution.py:17
  116.4 13.1 %collective-permute-start.7 = (f32[512,128]{1,0:T(8,128)S(1)}, f32[512,128]{1,0:T(8,128)S(1)}, u32[]{:S(2)}, u32[]{:S(2)}) collective-permute-start(f32[512,128]{1,0:T(8,128)S(1)} %pad_maximum_fusion.1), channel_id=1, source_target_pairs={{0,8},{1,9},{2,10},{3,11},{4,12},{5,13},{6,14},{7,15},{16,24},{17,... | collective-permute-start | bytes 786440 | tf_op jit(solution)/shard_map/ppermute | solution.py:17
  128.2 14.3 %collective-permute-start.22 = (bf16[1024,512]{1,0:T(8,128)(2,1)S(1)}, bf16[1024,512]{1,0:T(8,128)(2,1)S(1)}, u32[]{:S(2)}, u32[]{:S(2)}) collective-permute-start(bf16[1024,512]{1,0:T(8,128)(2,1)S(1)} %add_select_fusion), channel_id=1, source_target_pairs={{0,16},{32,48},{64,80},{96,112},{1,17},{33,49},{65,81},{97,113},{2... | collective-permute-start | bytes 3145736 | tf_op jit(solution)/shard_map/ppermute | solution.py:17
  129.6 2.7 %collective-permute-start.10 = (f32[512,128]{1,0:T(8,128)S(1)}, f32[512,128]{1,0:T(8,128)S(1)}, u32[]{:S(2)}, u32[]{:S(2)}) collective-permute-start(f32[512,128]{1,0:T(8,128)S(1)} %broadcast_select_fusion.2), channel_id=1, source_target_pairs={{0,96},{1,97},{2,98},{3,99},{4,100},{5,101},{6,102},{7,103},{8,104... | collective-permute-start | bytes 786440 | tf_op jit(solution)/shard_map/ppermute | solution.py:17
  130.3 2.0 %collective-permute-start.8 = (f32[512,128]{1,0:T(8,128)S(1)}, f32[512,128]{1,0:T(8,128)S(1)}, u32[]{:S(2)}, u32[]{:S(2)}) collective-permute-start(f32[512,128]{1,0:T(8,128)S(1)} %broadcast_select_fusion.2), channel_id=1, source_target_pairs={{0,64},{1,65},{2,66},{3,67},{4,68},{5,69},{6,70},{7,71},{8,72},{9,... | collective-permute-start | bytes 786440 | tf_op jit(solution)/shard_map/ppermute | solution.py:17
  131.0 8.3 %collective-permute-start.9 = (f32[512,128]{1,0:T(8,128)S(1)}, f32[512,128]{1,0:T(8,128)S(1)}, u32[]{:S(2)}, u32[]{:S(2)}) collective-permute-start(f32[512,128]{1,0:T(8,128)S(1)} %broadcast_select_fusion.2), channel_id=1, source_target_pairs={{0,32},{1,33},{2,34},{3,35},{4,36},{5,37},{6,38},{7,39},{8,40},{9,... | collective-permute-start | bytes 786440 | tf_op jit(solution)/shard_map/ppermute | solution.py:17
  139.3 2.4 %collective-permute-start.11 = (f32[512,128]{1,0:T(8,128)S(1)}, f32[512,128]{1,0:T(8,128)S(1)}, u32[]{:S(2)}, u32[]{:S(2)}) collective-permute-start(f32[512,128]{1,0:T(8,128)S(1)} %add_select_fusion.2), channel_id=1, source_target_pairs={{0,16},{32,48},{64,80},{96,112},{1,17},{33,49},{65,81},{97,113},{2... | collective-permute-start | bytes 786440 | tf_op jit(solution)/shard_map/ppermute | solution.py:17
  146.4 22.6 %collective-permute-start.23 = (f32[64,128]{1,0:T(8,128)}, f32[64,128]{1,0:T(8,128)S(1)}, u32[]{:S(2)}, u32[]{:S(2)}) collective-permute-start(f32[64,128]{1,0:T(8,128)} %shard_map.87), channel_id=1, source_target_pairs={{0,16},{16,32},{32,48},{48,64},{64,80},{80,96},{96,112},{1,17},{17... | collective-permute-start | bytes 98312 | tf_op jit(solution)/shard_map/ppermute | solution.py:17
  148.7 20.3 %collective-permute-start.24 = (f32[64,128]{1,0:T(8,128)}, f32[64,128]{1,0:T(8,128)S(1)}, u32[]{:S(2)}, u32[]{:S(2)}) collective-permute-start(f32[64,128]{1,0:T(8,128)} %shard_map.87), channel_id=1, source_target_pairs={{16,0},{32,16},{48,32},{64,48},{80,64},{96,80},{112,96},{17,1},{33... | collective-permute-start | bytes 98312 | tf_op jit(solution)/shard_map/ppermute | solution.py:17
  152.0 17.0 %collective-permute-start.25 = (f32[64,128]{1,0:T(8,128)}, f32[64,128]{1,0:T(8,128)S(1)}, u32[]{:S(2)}, u32[]{:S(2)}) collective-permute-start(f32[64,128]{1,0:T(8,128)} %shard_map.87), channel_id=1, source_target_pairs={{0,1},{1,2},{2,3},{3,4},{4,5},{5,6},{6,7},{7,8},{8,9},{9,10},{10,1... | collective-permute-start | bytes 98312 | tf_op jit(solution)/shard_map/ppermute | solution.py:17
  155.0 14.0 %collective-permute-start.26 = (f32[64,128]{1,0:T(8,128)}, f32[64,128]{1,0:T(8,128)S(1)}, u32[]{:S(2)}, u32[]{:S(2)}) collective-permute-start(f32[64,128]{1,0:T(8,128)} %shard_map.87), channel_id=1, source_target_pairs={{1,0},{2,1},{3,2},{4,3},{5,4},{6,5},{7,6},{8,7},{9,8},{10,9},{11,1... | collective-permute-start | bytes 98312 | tf_op jit(solution)/shard_map/ppermute | solution.py:17
  160.0 9.5 %copy-start.4 = (f32[64,128]{1,0:T(8,128)S(1)}, f32[64,128]{1,0:T(8,128)}, u32[]{:S(2)}) copy-start(f32[64,128]{1,0:T(8,128)} %shard_map.87) | copy-start | bytes 98308
  (5 other events, 35.8 us)
Sparse Core Ops, SparseCore 0:
  100.4 52.7 all-gather.2
